TPU v7x, 256 devices: a whole 4x4x8 slice. The times are simulated.
256 devices in a mesh: replica: 32 (over y, x, core), tensor: 8 (over z).
Axes of the slice: x: 4, y: 4, z: 8, core: 2. Of those that a mesh axis runs over, the one named last changes fastest.
Arguments:
- gate_grad: bfloat16 [32, 3072, 1024], P('replica', 'tensor'), may hold values from -16 to 16
- up_grad: bfloat16 [32, 3072, 1024], P('replica', 'tensor'), may hold values from -16 to 16
- down_grad: bfloat16 [32, 1024, 3072], P('replica', None, 'tensor'), may hold values from -16 to 16
- gate_error: bfloat16 [32, 3072, 1024], P('replica', 'tensor'), may hold values from -6 to 6
- up_error: bfloat16 [32, 3072, 1024], P('replica', 'tensor'), may hold values from -6 to 6
- down_error: bfloat16 [32, 1024, 3072], P('replica', None, 'tensor'), may hold values from -6 to 6
- q_init: float32 [3, 1024, 32], replicated, may hold values from -6 to 6
Outputs:
- gate_update: bfloat16 [3072, 1024], P('tensor')
- up_update: bfloat16 [3072, 1024], P('tensor')
- down_update: bfloat16 [1024, 3072], P(None, 'tensor')
- gate_error_next: bfloat16 [32, 3072, 1024], P('replica', 'tensor')
- up_error_next: bfloat16 [32, 3072, 1024], P('replica', 'tensor')
- down_error_next: bfloat16 [32, 1024, 3072], P('replica', None, 'tensor')
- q_next: float32 [3, 1024, 32], replicated
All inputs are finite; a program needn't handle non-finite values.
Results may differ from a plain program's by a relative error of at most 0.0015.
Values sent between devices are 32-bit elements; how exact they have to be, the bound alone decides.
A program may use at most 64 MiB of HBM per device.

v0:
```python
import jax
import jax.numpy as jnp
from jax import lax
from jax.sharding import PartitionSpec as P

ITERS = 2


HI = lax.Precision.HIGHEST


def project(matrix, which, q_now):
    if which == 2:
        return jnp.einsum("df,dk->fk", matrix, q_now, precision=HI)
    return jnp.einsum("fd,dk->fk", matrix, q_now, precision=HI)


def back_project(matrix, which, p_hat):
    if which == 2:
        return jnp.einsum("df,fk->dk", matrix, p_hat, precision=HI)
    return jnp.einsum("fd,fk->dk", matrix, p_hat, precision=HI)


def gram_of(pmat):
    return jnp.dot(pmat.T, pmat, precision=HI, preferred_element_type=jnp.float32)


def shards(gate_grad, up_grad, down_grad, gate_error, up_error, down_error, q_init):
    replicas = lax.axis_size("replica")
    mats = (
        gate_grad[0].astype(jnp.float32) + gate_error[0].astype(jnp.float32),
        up_grad[0].astype(jnp.float32) + up_error[0].astype(jnp.float32),
        down_grad[0].astype(jnp.float32) + down_error[0].astype(jnp.float32),
    )
    q_now = (q_init[0], q_init[1], q_init[2])
    for step in range(ITERS):
        terms = tuple((project(mats[i], i, q_now[i]) for i in range(3)))
        summed = lax.psum(terms, "replica")
        pmats = tuple((x / replicas for x in summed))
        grams = lax.psum(tuple((gram_of(x) for x in pmats)), "tensor")
        p_hats = tuple(
            (
                lax.linalg.triangular_solve(
                    jnp.linalg.cholesky(grams[i]),
                    pmats[i],
                    left_side=False,
                    lower=True,
                    transpose_a=True,
                )
                for i in range(3)
            )
        )
        q_terms = tuple((back_project(mats[i], i, p_hats[i]) for i in range(3)))
        q_total = lax.psum(q_terms, ("replica", "tensor"))
        q_now = tuple((x / replicas for x in q_total))
    updates = (
        jnp.dot(p_hats[0], q_now[0].T, precision=HI, preferred_element_type=jnp.float32),
        jnp.dot(p_hats[1], q_now[1].T, precision=HI, preferred_element_type=jnp.float32),
        jnp.dot(q_now[2], p_hats[2].T, precision=HI, preferred_element_type=jnp.float32),
    )
    errors = tuple(((mats[i] - updates[i]).astype(jnp.bfloat16)[None] for i in range(3)))
    return (
        updates[0].astype(jnp.bfloat16),
        updates[1].astype(jnp.bfloat16),
        updates[2].astype(jnp.bfloat16),
        errors[0],
        errors[1],
        errors[2],
        jnp.stack(q_now),
    )


def solution(mesh):
    in_specs = (
        P("replica", "tensor", None),
        P("replica", "tensor", None),
        P("replica", None, "tensor"),
        P("replica", "tensor", None),
        P("replica", "tensor", None),
        P("replica", None, "tensor"),
        P(),
    )
    out_specs = (
        P("tensor", None),
        P("tensor", None),
        P(None, "tensor"),
        P("replica", "tensor", None),
        P("replica", "tensor", None),
        P("replica", None, "tensor"),
        P(),
    )
    return jax.shard_map(shards, mesh=mesh, in_specs=in_specs, out_specs=out_specs, check_vma=False)
```

profile of v0, /device:TPU:1, one launch (start us, length us, event | category | flops | bytes accessed | tf_op | source)
XLA Modules:
  0.0 878.5 jit_solution(2253279083001234744)
XLA Ops:
  7.2 3.7 fusion.24
  11.0 2.7 fusion.6
  13.7 3.1 fusion.15
  16.9 113.1 %all-reduce.17.cloned.1.call-done = (f32[384,32]{0,1:T(8,128)}, f32[384,32]{0,1:T(8,128)}, f32[384,32]{0,1:T(8,128)}) async-done(((f32[384,32]{0,1:T(8,128)}, f32[384,32]{0,1:T(8,128)}, f32[384,32]{0,1:T(8,128)}), (f32[384,32]{0,1:T(8,128)}, f32[384,32]{0,1:T(8,128)}, f32[384,32]{0,1:T(8,128)})) %all-reduce.17.cloned.1.call-update) | async-done | bytes 147472 | tf_op jit(solution)/shard_map/psum | solution.py:38
  133.2 24.2 %all-reduce.5 = (f32[32,32]{0,1:T(8,128)S(1)}, f32[32,32]{0,1:T(8,128)S(1)}, f32[32,32]{0,1:T(8,128)S(1)}) all-reduce(f32[32,32]{0,1:T(8,128)S(1)} %fusion.67, f32[32,32]{0,1:T(8,128)S(1)} %fusion.61, f32[32,32]{0,1:T(8,128)S(1)} %fusion.55), channel_id=1, replica_groups=mesh['replica'=32,'tensor'=8] {'tensor'}, use_global_device_ids=true, to_apply=%region_1.0 | all-reduce | flops 3072 | bytes 24576 | tf_op jit(solution)/shard_map/psum | solution.py:40
  157.5 2.9 cholesky.104
  161.7 2.4 custom-call.10
  165.4 2.9 cholesky.148
  169.6 2.4 custom-call.14
  173.2 2.9 cholesky.126
  177.4 2.4 custom-call.12
  186.4 251.2 %all-reduce.13.cloned.1.call-done = (f32[1024,32]{0,1:T(8,128)}, f32[1024,32]{0,1:T(8,128)}, f32[1024,32]{0,1:T(8,128)}) async-done(((f32[1024,32]{0,1:T(8,128)}, f32[1024,32]{0,1:T(8,128)}, f32[1024,32]{0,1:T(8,128)}), (f32[1024,32]{0,1:T(8,128)}, f32[1024,32]{0,1:T(8,128)}, f32[1024,32]{0,1:T(8,128)})) %all-reduce.13.cloned.1.call-update) | async-done | bytes 393232 | tf_op jit(solution)/shard_map/psum | solution.py:54
  437.6 3.7 fusion.20
  445.4 108.1 %all-reduce.15.cloned.1.call-done = (f32[384,32]{0,1:T(8,128)}, f32[384,32]{0,1:T(8,128)}, f32[384,32]{0,1:T(8,128)}) async-done(((f32[384,32]{0,1:T(8,128)}, f32[384,32]{0,1:T(8,128)}, f32[384,32]{0,1:T(8,128)}), (f32[384,32]{0,1:T(8,128)}, f32[384,32]{0,1:T(8,128)}, f32[384,32]{0,1:T(8,128)})) %all-reduce.15.cloned.1.call-update) | async-done | bytes 147472 | tf_op jit(solution)/shard_map/psum | solution.py:38
  556.7 24.2 %all-reduce.4 = (f32[32,32]{0,1:T(8,128)S(1)}, f32[32,32]{0,1:T(8,128)S(1)}, f32[32,32]{0,1:T(8,128)S(1)}) all-reduce(f32[32,32]{0,1:T(8,128)S(1)} %fusion.64, f32[32,32]{0,1:T(8,128)S(1)} %fusion.58, f32[32,32]{0,1:T(8,128)S(1)} %fusion.52), channel_id=1, replica_groups=mesh['replica'=32,'tensor'=8] {'tensor'}, use_global_device_ids=true, to_apply=%region_6.9 | all-reduce | flops 3072 | bytes 24576 | tf_op jit(solution)/shard_map/psum | solution.py:40
  580.9 2.9 cholesky.115
  585.2 2.4 custom-call.11
  588.8 2.9 cholesky.137
  593.0 2.4 custom-call.13
  596.6 2.9 cholesky.159
  609.6 251.5 %all-reduce.11.cloned.1.call-done = (f32[1024,32]{0,1:T(8,128)}, f32[1024,32]{0,1:T(8,128)}, f32[1024,32]{0,1:T(8,128)}) async-done(((f32[1024,32]{0,1:T(8,128)}, f32[1024,32]{0,1:T(8,128)}, f32[1024,32]{0,1:T(8,128)}), (f32[1024,32]{0,1:T(8,128)}, f32[1024,32]{0,1:T(8,128)}, f32[1024,32]{0,1:T(8,128)})) %all-reduce.11.cloned.1.call-update) | async-done | bytes 393232 | tf_op jit(solution)/shard_map/psum | solution.py:54
  862.0 3.7 fusion.29
  865.7 2.7 fusion.28
  868.5 2.7 fusion.27
  (94 shorter events, 40.2 us)
Async XLA Ops:
  7.2 3.8 copy-start
  7.2 3.8 copy-start.1
  7.2 122.8 %all-reduce.17.cloned.1.call-start = ((), (), s32[]{:S(2)}) async-start(), calls=%async_computation.3 | async-start | bytes 294912 | tf_op jit(solution)/shard_map/psum | solution.py:38
  11.0 2.8 copy-start.2
  11.0 2.8 copy-start.3
  16.9 420.7 %all-reduce.13.cloned.1.call-start = ((), (), s32[]{:S(2)}) async-start(), calls=%async_computation.1 | async-start | bytes 786432 | tf_op jit(solution)/shard_map/psum | solution.py:54
  130.0 49.8 %copy-start.12 = (f32[384,32]{0,1:T(8,128)S(1)}, f32[384,32]{0,1:T(8,128)}, u32[]{:S(2)}) copy-start(f32[384,32]{0,1:T(8,128)} %get-tuple-element.19) | copy-start | bytes 147460
  181.9 2.4 copy-start.4
  181.9 2.4 copy-start.7
  186.2 367.3 %all-reduce.15.cloned.1.call-start = ((), (), s32[]{:S(2)}) async-start(), calls=%async_computation.2 | async-start | bytes 294912 | tf_op jit(solution)/shard_map/psum | solution.py:38
  437.6 3.7 copy-start.15
  441.3 2.3 copy-start.14
  445.3 415.8 %all-reduce.11.cloned.1.call-start = ((), (), s32[]{:S(2)}) async-start(), calls=%async_computation | async-start | bytes 786432 | tf_op jit(solution)/shard_map/psum | solution.py:54
  553.5 49.8 %copy-start.13 = (f32[384,32]{0,1:T(8,128)S(1)}, f32[384,32]{0,1:T(8,128)}, u32[]{:S(2)}) copy-start(f32[384,32]{0,1:T(8,128)} %get-tuple-element.17) | copy-start | bytes 147460
  606.0 1.8 copy-start.5
  606.0 1.8 copy-start.8
  862.0 3.7 copy-start.11
  865.7 2.8 copy-start.10
  865.7 2.8 copy-start.6
  865.7 2.8 copy-start.9
Sparse Core Ops, SparseCore 0:
  17.0 112.9 all-reduce.16
  186.3 251.3 all-reduce.12
  445.4 107.9 all-reduce.14
  609.7 251.2 all-reduce.10
where the time goes:
time: 879 us
  waiting for transfers between devices  724 us (82%)
  matrix products  49.6 us (6%)
  blocking collectives  48.3 us (5%)
  other arithmetic  41.8 us (5%)
  between operations  14.1 us (2%)
    psum x2, waiting for transfers between devices, shards(): q_total = lax.psum(q_terms, ('replica', 'tensor'))  503 us
    psum x2, waiting for transfers between devices, shards(): summed = lax.psum(terms, 'replica')  221 us
    psum x2, blocking collectives, shards(): grams = lax.psum(tuple((gram_of(x) for x in pmats)), 'tensor')  48.3 us
    another operation x18, other arithmetic, shards(): jnp.linalg.cholesky(grams[i])  21.6 us
    another operation x12, other arithmetic, shards(): lax.linalg.triangular_solve(jnp.linalg.cholesky(grams[i]), pmats[i], left...  18.5 us
  transfers between devices with their start and end apart: 4, of which 4 were waited for; matrix products, arithmetic and copies ran while one was open for 0% of the time, Pallas kernels for 0%

commit v1 on v0

v1 whole, which is shorter than its diff:
```python
import jax
import jax.numpy as jnp
from jax import lax
from jax.experimental import pallas as pl
from jax.experimental.pallas import tpu as pltpu
from jax.sharding import PartitionSpec as P

ITERS = 2
D = 1024
RANK = 32
ROWS = 384
NY, NX, NZ = 4, 4, 8
MESH = pl.DeviceIdType.MESH
F32 = jnp.float32
BF16 = jnp.bfloat16
PARTS = 2

P_CORE, P_ONE, P_TWO, P_BACK, GRAM, Q_CORE, Q_SCATTER, Q_Z, Q_GATHER, Q_BACK = range(10)


def split(x, parts):
    out = []
    for k in range(parts):
        piece = x.astype(BF16)
        out.append(piece)
        if k + 1 < parts:
            x = x - piece.astype(F32)
    return out


def dot(a, b, ca, cb):
    return lax.dot_general(a, b, (((ca,), (cb,)), ((), ())), preferred_element_type=F32)


def small_left(a, cat_axis):
    h, m, l = split(a, 3)
    return jnp.concatenate([h, h, m, h, l, m], axis=cat_axis)


def small_right(b):
    h, m, l = split(b, 3)
    return jnp.concatenate([h, m, h, l, h, m], axis=0)


def fold(x, parts):
    total = x[(parts - 1) * RANK :]
    for k in range(parts - 2, -1, -1):
        total = total + x[k * RANK : (k + 1) * RANK]
    return total


def inverse_factors(grams):
    row = lax.broadcasted_iota(jnp.int32, (RANK, 2 * RANK), 0)
    lane = lax.broadcasted_iota(jnp.int32, (RANK, 2 * RANK), 1)
    eye = (lane == row + RANK).astype(F32)
    augs = []
    for g in grams:
        augs.append(jnp.concatenate([g, jnp.zeros_like(g)], axis=1) + eye)
    for j in range(RANK):
        for n in range(len(augs)):
            a = augs[n]
            pivot = a[j : j + 1, j : j + 1]
            r = lax.rsqrt(pivot)
            r = r * (1.5 - 0.5 * pivot * r * r)
            top = a[j : j + 1, :] * r
            col = a[:, j : j + 1] * r
            a = jnp.where(row > j, a - col * top, jnp.where(row == j, top, a))
            augs[n] = a
    return [a[:, RANK:] for a in augs]


def kernel(
    g0, g1, g2, e0, e1, e2, q0,
    q_out, ps_out, qs_out,
    gm, em, gd, ed, qs, pt, pc, x1, x2, pf, gz, qp, qc, qsum, qr, zq, qf, linv,
    load, ssem, rsem,
):
    r = lax.axis_index("replica")
    z = lax.axis_index("tensor")
    y, x, c = r // 8, (r // 2) % 4, r % 2
    p = y * 4 + x
    other = 1 - c
    sib = (y * 8 + x * 2 + other, z)

    def at(yy, xx):
        return (yy * 8 + xx * 2 + c, z)

    plane = [
        ((y + dy) % NY, (x + dx) % NX)
        for dy, dx in [
            (2, 2), (2, 1), (1, 2), (2, 3), (3, 2), (1, 1), (1, 3), (3, 1), (3, 3),
            (2, 0), (0, 2), (1, 0), (0, 1), (3, 0), (0, 3),
        ]
    ]
    column = [(r, (z + dz) % NZ) for dz in (4, 3, 5, 2, 6, 1, 7)]
    xs = [at(y, (x + d) % NX) for d in (2, 1, 3)]
    ys = [at((y + d) % NY, x) for d in (2, 1, 3)]

    barrier = pltpu.get_barrier_semaphore()
    greet = [at(yy, xx) for yy, xx in plane] + column + [sib]
    for dev in greet:
        pl.semaphore_signal(barrier, inc=1, device_id=dev, device_id_type=MESH)

    loads = []
    for i, (src, dst) in enumerate(
        [(g0, gm.at[0]), (e0, em.at[0]), (g1, gm.at[1]), (e1, em.at[1]), (g2, gd), (e2, ed)]
    ):
        cp = pltpu.make_async_copy(src, dst, load.at[i])
        cp.start()
        loads.append(cp)

    def send(stage, t, i, src, dst, dev):
        pltpu.make_async_remote_copy(
            src_ref=src,
            dst_ref=dst,
            send_sem=ssem.at[stage, t],
            recv_sem=rsem.at[stage, t, i],
            device_id=dev,
            device_id_type=MESH,
        ).start()

    def arrived(stage, t, i, like):
        pltpu.make_async_copy(like, like, rsem.at[stage, t, i]).wait()

    for i in range(3):
        qs[i] = jnp.concatenate(split(q0[i], PARTS), axis=0)

    def project(i):
        if i == 2:
            v = dot(qs[i], gd[...], 1, 0) + dot(qs[i], ed[...], 1, 0)
        else:
            v = dot(qs[i], gm[i], 1, 1) + dot(qs[i], em[i], 1, 1)
        return fold(v, PARTS) * (1.0 / 32.0)

    def back_project(i, ps):
        if i == 2:
            v = dot(ps, gd[...], 1, 1) + dot(ps, ed[...], 1, 1)
        else:
            v = dot(ps, gm[i], 1, 0) + dot(ps, em[i], 1, 0)
        return fold(v, PARTS) * (1.0 / 32.0)

    def iteration(t, first):
        for i in range(3):
            if first:
                loads[2 * i].wait()
                loads[2 * i + 1].wait()
            pt[t, i] = project(i).reshape(4, 8, ROWS)
            if first and i == 0:
                pl.semaphore_wait(barrier, len(greet))
            send(P_CORE, t, i, pt.at[t, i, pl.ds(2 * other, 2)], pc.at[t, i], sib)
        for i in range(3):
            arrived(P_CORE, t, i, pc.at[t, i])
            s = pt[t, i, pl.ds(2 * c, 2)] + pc[t, i]
            x1[t, i, 0, x] = s[0]
            x1[t, i, 1, y] = s[1]
            for dev in xs:
                send(P_ONE, t, i, x1.at[t, i, 0, x], x1.at[t, i, 0, x], dev)
            for dev in ys:
                send(P_ONE, t, i, x1.at[t, i, 1, y], x1.at[t, i, 1, y], dev)
        for i in range(3):
            arrived(P_ONE, t, i, x1.at[t, i, :, pl.ds(0, 3)])
            a = (x1[t, i, 0, 0] + x1[t, i, 0, 1]) + (x1[t, i, 0, 2] + x1[t, i, 0, 3])
            b = (x1[t, i, 1, 0] + x1[t, i, 1, 1]) + (x1[t, i, 1, 2] + x1[t, i, 1, 3])
            x2[t, i, 0, y] = a
            x2[t, i, 1, x] = b
            for dev in ys:
                send(P_TWO, t, i, x2.at[t, i, 0, y], x2.at[t, i, 0, y], dev)
            for dev in xs:
                send(P_TWO, t, i, x2.at[t, i, 1, x], x2.at[t, i, 1, x], dev)
        for i in range(3):
            arrived(P_TWO, t, i, x2.at[t, i, :, pl.ds(0, 3)])
            a = (x2[t, i, 0, 0] + x2[t, i, 0, 1]) + (x2[t, i, 0, 2] + x2[t, i, 0, 3])
            b = (x2[t, i, 1, 0] + x2[t, i, 1, 1]) + (x2[t, i, 1, 2] + x2[t, i, 1, 3])
            pf[t, i, 2 * c] = a
            pf[t, i, 2 * c + 1] = b
            send(P_BACK, t, i, pf.at[t, i, pl.ds(2 * c, 2)], pf.at[t, i, pl.ds(2 * c, 2)], sib)
        grams = []
        for i in range(3):
            arrived(P_BACK, t, i, pf.at[t, i, pl.ds(0, 2)])
            ps = jnp.concatenate(split(pf[t, i].reshape(RANK, ROWS), PARTS), axis=0)
            term = back_project(i, ps)
            qp[t, i] = term.reshape(2, 2, 8, D)
            send(Q_CORE, t, i, qp.at[t, i, other], qc.at[t, i], sib)
            gg = fold(dot(ps, ps, 1, 1), PARTS)
            gram = gg[:, (PARTS - 1) * RANK :]
            for k in range(PARTS - 2, -1, -1):
                gram = gram + gg[:, k * RANK : (k + 1) * RANK]
            grams.append(gram)
        gz[t, z] = jnp.concatenate(grams + [jnp.zeros((RANK, RANK), F32)], axis=1)
        for dev in column:
            send(GRAM, t, 0, gz.at[t, z], gz.at[t, z], dev)
        for i in range(3):
            arrived(Q_CORE, t, i, qc.at[t, i])
            s = qp[t, i, c] + qc[t, i]
            for k in range(16):
                qsum[t, i, k] = s[k // 8, :, (k % 8) * 128 : (k % 8 + 1) * 128]
            qr[t, i, p] = qsum[t, i, p]
            for yy, xx in plane:
                send(Q_SCATTER, t, i, qsum.at[t, i, yy * 4 + xx], qr.at[t, i, p], at(yy, xx))
        for i in range(3):
            arrived(Q_SCATTER, t, i, qr.at[t, i, pl.ds(0, 15)])
            zq[t, i, z] = jnp.sum(qr[t, i], axis=0)
            for dev in column:
                send(Q_Z, t, i, zq.at[t, i, z], zq.at[t, i, z], dev)
        arrived(GRAM, t, 0, gz.at[t, pl.ds(0, 7)])
        gram = jnp.sum(gz[t], axis=0)
        inv = inverse_factors([gram[:, k * RANK : (k + 1) * RANK] for k in range(3)])
        for i in range(3):
            linv[i] = small_left(inv[i], 1)
        for i in range(3):
            arrived(Q_Z, t, i, zq.at[t, i, pl.ds(0, 7)])
            qf[t, i, c, p] = jnp.sum(zq[t, i], axis=0)
            for yy, xx in plane:
                send(Q_GATHER, t, i, qf.at[t, i, c, p], qf.at[t, i, c, p], at(yy, xx))
        for i in range(3):
            arrived(Q_GATHER, t, i, qf.at[t, i, 0, pl.ds(0, 15)])
            send(Q_BACK, t, i, qf.at[t, i, c], qf.at[t, i, c], sib)
        for i in range(3):
            arrived(Q_BACK, t, i, qf.at[t, i, 0])
            full = qf[t, i]
            raw = jnp.concatenate(
                [
                    jnp.concatenate([full[k // 2, (k % 2) * 8 + l] for l in range(8)], axis=1)
                    for k in range(4)
                ],
                axis=0,
            )
            q_now = dot(linv[i], small_right(raw), 1, 0)
            if first:
                qs[i] = jnp.concatenate(split(q_now, PARTS), axis=0)
            else:
                q_out[i] = q_now
                qh, ql = split(q_now, 2)
                qs_out[i] = jnp.concatenate([qh, ql, qh], axis=0)
                p_hat = dot(linv[i], small_right(pf[t, i].reshape(RANK, ROWS)), 1, 0)
                ph, pw = split(p_hat, 2)
                ps_out[i] = jnp.concatenate([ph, ph, pw], axis=0)

    for t in range(ITERS):
        iteration(t, t == 0)

    def sent(stage, t, like):
        pltpu.make_async_copy(like, like, ssem.at[stage, t]).wait()

    for t in range(ITERS):
        sent(P_CORE, t, pc.at[t])
        sent(P_ONE, t, x1.at[t, :, :, pl.ds(0, 3)])
        sent(P_TWO, t, x2.at[t, :, :, pl.ds(0, 3)])
        sent(P_BACK, t, pf.at[t, :, pl.ds(0, 2)])
        sent(GRAM, t, gz.at[t, pl.ds(0, 7)])
        sent(Q_CORE, t, qc.at[t])
        sent(Q_SCATTER, t, qr.at[t, :, pl.ds(0, 15)])
        sent(Q_Z, t, zq.at[t, :, pl.ds(0, 7)])
        sent(Q_GATHER, t, qf.at[t, :, 0, pl.ds(0, 15)])
        sent(Q_BACK, t, qf.at[t, :, 0])


def exchange(grads, errors, q0):
    vmem = lambda *shape: pltpu.VMEM(shape, F32)
    scratch = [
        pltpu.VMEM((2, ROWS, D), BF16),
        pltpu.VMEM((2, ROWS, D), BF16),
        pltpu.VMEM((D, ROWS), BF16),
        pltpu.VMEM((D, ROWS), BF16),
        pltpu.VMEM((3, PARTS * RANK, D), BF16),
        vmem(ITERS, 3, 4, 8, ROWS),
        vmem(ITERS, 3, 2, 8, ROWS),
        vmem(ITERS, 3, 2, 4, 8, ROWS),
        vmem(ITERS, 3, 2, 4, 8, ROWS),
        vmem(ITERS, 3, 4, 8, ROWS),
        vmem(ITERS, NZ, RANK, 128),
        vmem(ITERS, 3, 2, 2, 8, D),
        vmem(ITERS, 3, 2, 8, D),
        vmem(ITERS, 3, 16, 8, 128),
        vmem(ITERS, 3, 16, 8, 128),
        vmem(ITERS, 3, NZ, 8, 128),
        vmem(ITERS, 3, 2, 16, 8, 128),
        pltpu.VMEM((3, RANK, 6 * RANK), BF16),
        pltpu.SemaphoreType.DMA((6,)),
        pltpu.SemaphoreType.DMA((10, ITERS)),
        pltpu.SemaphoreType.DMA((10, ITERS, 3)),
    ]
    anywhere = pl.BlockSpec(memory_space=pl.ANY)
    inside = pl.BlockSpec(memory_space=pltpu.VMEM)
    return pl.pallas_call(
        kernel,
        name="power",
        out_shape=(
            jax.ShapeDtypeStruct((3, RANK, D), F32),
            jax.ShapeDtypeStruct((3, 3 * RANK, ROWS), BF16),
            jax.ShapeDtypeStruct((3, 3 * RANK, D), BF16),
        ),
        in_specs=[anywhere] * 6 + [inside],
        out_specs=(inside, inside, inside),
        scratch_shapes=scratch,
        compiler_params=pltpu.CompilerParams(
            collective_id=0, has_side_effects=True, vmem_limit_bytes=32 << 20
        ),
        cost_estimate=pl.CostEstimate(flops=10**9, bytes_accessed=6 * 10**6, transcendentals=0),
    )(*grads, *errors, q0)


STEPS = 4
WIDE = D // STEPS


def finish_kernel(ps, qs, q, g0, g1, g2, e0, e1, e2, u0, u1, u2, n0, n1, n2, q_out):
    def one(g, e, u, n, left, right):
        v = dot(left, right, 0, 0)
        u[...] = v.astype(BF16)
        n[...] = ((g[...].astype(F32) + e[...].astype(F32)) - v).astype(BF16)

    one(g0, e0, u0, n0, ps[0], qs[0])
    one(g1, e1, u1, n1, ps[1], qs[1])
    one(g2, e2, u2, n2, qs[2], ps[2])
    q_out[...] = q[...]


def finish(ps, qs, q, grads, errors):
    tall = pl.BlockSpec((ROWS, WIDE), lambda s: (0, s))
    flat = pl.BlockSpec((WIDE, ROWS), lambda s: (s, 0))
    q_spec = pl.BlockSpec((3, RANK, WIDE), lambda s: (0, 0, s))
    shapes = [(ROWS, D), (ROWS, D), (D, ROWS)]
    outs = [jax.ShapeDtypeStruct(shape, BF16) for shape in shapes]
    return pl.pallas_call(
        finish_kernel,
        name="finish",
        grid=(STEPS,),
        in_specs=[
            pl.BlockSpec((3, 3 * RANK, ROWS), lambda s: (0, 0, 0)),
            pl.BlockSpec((3, 3 * RANK, WIDE), lambda s: (0, 0, s)),
            q_spec,
            tall, tall, flat, tall, tall, flat,
        ],
        out_specs=[tall, tall, flat, tall, tall, flat, q_spec],
        out_shape=outs + outs + [jax.ShapeDtypeStruct((3, RANK, D), F32)],
        compiler_params=pltpu.CompilerParams(vmem_limit_bytes=32 << 20),
    )(ps, qs, q, *grads, *errors)


def shards(gate_grad, up_grad, down_grad, gate_error, up_error, down_error, q_init):
    grads = (gate_grad[0], up_grad[0], down_grad[0])
    errors = (gate_error[0], up_error[0], down_error[0])
    q, ps, qs = exchange(grads, errors, jnp.swapaxes(q_init, 1, 2))
    u0, u1, u2, n0, n1, n2, q_next = finish(ps, qs, q, grads, errors)
    return u0, u1, u2, n0[None], n1[None], n2[None], jnp.swapaxes(q_next, 1, 2)


def solution(mesh):
    in_specs = (
        P("replica", "tensor", None),
        P("replica", "tensor", None),
        P("replica", None, "tensor"),
        P("replica", "tensor", None),
        P("replica", "tensor", None),
        P("replica", None, "tensor"),
        P(),
    )
    out_specs = (
        P("tensor", None),
        P("tensor", None),
        P(None, "tensor"),
        P("replica", "tensor", None),
        P("replica", "tensor", None),
        P("replica", None, "tensor"),
        P(),
    )
    return jax.shard_map(shards, mesh=mesh, in_specs=in_specs, out_specs=out_specs, check_vma=False)
```

time: 879 us -> 79.5 us (0.09)
  waiting for transfers between devices: 724 us -> 0 us
  Pallas kernels: 0 us -> 70.7 us
  matrix products: 49.6 us -> 0 us
  blocking collectives: 48.3 us -> 0 us
  other arithmetic: 41.8 us -> 0 us
  between operations: 14.1 us -> 0.66 us
    psum x4 -> x0, waiting for transfers between devices: 724 us -> none  [the longest x2 503 us: shards(): q_total = lax.psum(q_terms, ('replica', 'tensor'))]
    pallas_call x0 -> x2, Pallas kernels: none -> 70.7 us  [the longest x1 67.1 us: exchange(): pl.pallas_call(kernel, name='power', out_shape=(jax.ShapeDtypeStruct((3,...]
    psum x2 -> x0, blocking collectives: 48.3 us -> none  [shards(): grams = lax.psum(tuple((gram_of(x) for x in pmats)), 'tensor')]
    dot_general x21 -> x0, matrix products: 44.7 us -> none  [the longest x4 12.8 us: project(): return jnp.einsum('fd,dk->fk', matrix, q_now, precision=HI)]
    another operation x34 -> x0, other arithmetic: 41.8 us -> none  [the longest x18 21.6 us: shards(): jnp.linalg.cholesky(grams[i])]
  transfers between devices with their start and end apart: 4 -> 0, of which waited for: 4 -> 0; matrix products, arithmetic and copies ran while one was open for 0% -> 0% of each run, Pallas kernels for 0% -> 0%
where the time goes in v1:
time: 79.5 us; the launch traced here: 79.2 us
  Pallas kernels  70.7 us (89%)
  local copies, waits for them, and re-layouts  7.78 us (10%)
    pallas_call x1, Pallas kernels, exchange(): pl.pallas_call(kernel, name='power', out_shape=(jax.ShapeDtypeStruct((3,...  67.1 us
    unnamed x14, local copies, waits for them, and re-layouts  7.78 us
    pallas_call x1, Pallas kernels, finish(): pl.pallas_call(finish_kernel, name='finish', grid=(STEPS,), in_specs=[pl....  3.57 us

profile of v1, /device:TPU:1, one launch (start us, length us, event | category | flops | bytes accessed | tf_op | source)
XLA Modules:
  0.0 79.2 jit_solution(9832635505087133073)
XLA Ops:
  0.6 0.0 copy-start
  0.6 1.1 %copy-done = bf16[1,384,1024]{2,1,0:T(8,128)(2,1)S(1)} copy-done((bf16[1,384,1024]{2,1,0:T(8,128)(2,1)S(1)}, bf16[1,384,1024]{2,1,0:T(8,128)(2,1)}, u32[]{:S(2)}) %copy-start) | copy-done | bytes 786456
  1.8 0.0 copy-start.1
  1.8 1.1 %copy-done.1 = bf16[1,384,1024]{2,1,0:T(8,128)(2,1)S(1)} copy-done((bf16[1,384,1024]{2,1,0:T(8,128)(2,1)S(1)}, bf16[1,384,1024]{2,1,0:T(8,128)(2,1)}, u32[]{:S(2)}) %copy-start.1) | copy-done | bytes 786456
  2.9 0.0 copy-start.2
  2.9 1.1 %copy-done.2 = bf16[1,1024,384]{2,1,0:T(8,128)(2,1)S(1)} copy-done((bf16[1,1024,384]{2,1,0:T(8,128)(2,1)S(1)}, bf16[1,1024,384]{2,1,0:T(8,128)(2,1)}, u32[]{:S(2)}) %copy-start.2) | copy-done | bytes 786456
  4.0 0.0 copy-start.3
  4.0 1.1 %copy-done.3 = bf16[1,384,1024]{2,1,0:T(8,128)(2,1)S(1)} copy-done((bf16[1,384,1024]{2,1,0:T(8,128)(2,1)S(1)}, bf16[1,384,1024]{2,1,0:T(8,128)(2,1)}, u32[]{:S(2)}) %copy-start.3) | copy-done | bytes 786456
  5.2 0.0 copy-start.4
  5.2 1.1 %copy-done.4 = bf16[1,384,1024]{2,1,0:T(8,128)(2,1)S(1)} copy-done((bf16[1,384,1024]{2,1,0:T(8,128)(2,1)S(1)}, bf16[1,384,1024]{2,1,0:T(8,128)(2,1)}, u32[]{:S(2)}) %copy-start.4) | copy-done | bytes 786456
  6.3 0.0 copy-start.5
  6.3 1.1 %copy-done.5 = bf16[1,1024,384]{2,1,0:T(8,128)(2,1)S(1)} copy-done((bf16[1,1024,384]{2,1,0:T(8,128)(2,1)S(1)}, bf16[1,1024,384]{2,1,0:T(8,128)(2,1)}, u32[]{:S(2)}) %copy-start.5) | copy-done | bytes 786456
  7.4 0.0 copy-start.6
  7.4 1.0 %copy-done.6 = f32[3,1024,32]{1,2,0:T(8,128)S(1)} copy-done((f32[3,1024,32]{1,2,0:T(8,128)S(1)}, f32[3,1024,32]{1,2,0:T(8,128)}, u32[]{:S(2)}) %copy-start.6) | copy-done | bytes 393240
  8.4 67.1 %power.1 = (f32[3,32,1024]{2,1,0:T(8,128)S(1)}, bf16[3,96,384]{2,1,0:T(8,128)(2,1)S(1)}, bf16[3,96,1024]{2,1,0:T(8,128)(2,1)S(1)}) custom-call(bf16[384,1024]{1,0:T(8,128)(2,1)S(1)} %bitcast.11, bf16[384,1024]{1,0:T(8,128)(2,1)S(1)} %bitcast.13, bf16[1024,384]{1,0:T(8,128)(2,1)S(1)} %bitcast.15, bf16[384,1024]{1,0:T(8,128)(2,1)S(1)} %bitcast.17, ...), custom_call_target="tpu_custom_call" | custom-call | flops 1000000000 | bytes 6000000 | tf_op jit(solution)/shard_map/power/pallas_call | solution.py:285
  75.6 3.6 %finish.1 = (bf16[384,1024]{1,0:T(8,128)(2,1)}, bf16[384,1024]{1,0:T(8,128)(2,1)}, bf16[1024,384]{1,0:T(8,128)(2,1)}, bf16[384,1024]{1,0:T(8,128)(2,1)}, bf16[38...) custom-call(bf16[3,96,384]{2,1,0:T(8,128)(2,1)S(1)} %get-tuple-element.17.ps, ...), custom_call_target="tpu_custom_call" | custom-call | tf_op jit(solution)/shard_map/finish/pallas_call | solution.py:325
Async XLA Ops:
  0.6 1.1 %copy-start = (bf16[1,384,1024]{2,1,0:T(8,128)(2,1)S(1)}, bf16[1,384,1024]{2,1,0:T(8,128)(2,1)}, u32[]{:S(2)}) copy-start(bf16[1,384,1024]{2,1,0:T(8,128)(2,1)} %param.7) | copy-start | bytes 2359300
  1.8 1.1 %copy-start.1 = (bf16[1,384,1024]{2,1,0:T(8,128)(2,1)S(1)}, bf16[1,384,1024]{2,1,0:T(8,128)(2,1)}, u32[]{:S(2)}) copy-start(bf16[1,384,1024]{2,1,0:T(8,128)(2,1)} %param.8) | copy-start | bytes 2359300
  2.9 1.1 %copy-start.2 = (bf16[1,1024,384]{2,1,0:T(8,128)(2,1)S(1)}, bf16[1,1024,384]{2,1,0:T(8,128)(2,1)}, u32[]{:S(2)}) copy-start(bf16[1,1024,384]{2,1,0:T(8,128)(2,1)} %param.9) | copy-start | bytes 2359300
  4.0 1.1 %copy-start.3 = (bf16[1,384,1024]{2,1,0:T(8,128)(2,1)S(1)}, bf16[1,384,1024]{2,1,0:T(8,128)(2,1)}, u32[]{:S(2)}) copy-start(bf16[1,384,1024]{2,1,0:T(8,128)(2,1)} %param.10) | copy-start | bytes 2359300
  5.2 1.1 %copy-start.4 = (bf16[1,384,1024]{2,1,0:T(8,128)(2,1)S(1)}, bf16[1,384,1024]{2,1,0:T(8,128)(2,1)}, u32[]{:S(2)}) copy-start(bf16[1,384,1024]{2,1,0:T(8,128)(2,1)} %param.11) | copy-start | bytes 2359300
  6.3 1.1 %copy-start.5 = (bf16[1,1024,384]{2,1,0:T(8,128)(2,1)S(1)}, bf16[1,1024,384]{2,1,0:T(8,128)(2,1)}, u32[]{:S(2)}) copy-start(bf16[1,1024,384]{2,1,0:T(8,128)(2,1)} %param.12) | copy-start | bytes 2359300
  7.4 1.0 %copy-start.6 = (f32[3,1024,32]{1,2,0:T(8,128)S(1)}, f32[3,1024,32]{1,2,0:T(8,128)}, u32[]{:S(2)}) copy-start(f32[3,1024,32]{1,2,0:T(8,128)} %param.13) | copy-start | bytes 1179652

commit v2 on v1

--- a/solution.py
+++ b/solution.py
@@ -71,8 +71,8 @@
 
 def kernel(
     g0, g1, g2, e0, e1, e2, q0,
-    q_out, ps_out, qs_out,
-    gm, em, gd, ed, qs, pt, pc, x1, x2, pf, gz, qp, qc, qsum, qr, zq, qf, linv,
+    q_out, ps_out, qs_out, gm, em, gd, ed,
+    qi, qs, pt, pc, x1, x2, pf, gz, qp, qc, qsum, qr, zq, qf, linv,
     load, ssem, rsem,
 ):
     r = lax.axis_index("replica")
@@ -103,11 +103,12 @@
 
     loads = []
     for i, (src, dst) in enumerate(
-        [(g0, gm.at[0]), (e0, em.at[0]), (g1, gm.at[1]), (e1, em.at[1]), (g2, gd), (e2, ed)]
+        [(g0, gm.at[0]), (e0, em.at[0]), (g1, gm.at[1]), (e1, em.at[1]), (g2, gd), (e2, ed), (q0, qi)]
     ):
         cp = pltpu.make_async_copy(src, dst, load.at[i])
-        cp.start()
         loads.append(cp)
+    for k in (6, 0, 1, 2, 3, 4, 5):
+        loads[k].start()
 
     def send(stage, t, i, src, dst, dev):
         pltpu.make_async_remote_copy(
@@ -122,8 +123,9 @@
     def arrived(stage, t, i, like):
         pltpu.make_async_copy(like, like, rsem.at[stage, t, i]).wait()
 
+    loads[6].wait()
     for i in range(3):
-        qs[i] = jnp.concatenate(split(q0[i], PARTS), axis=0)
+        qs[i] = jnp.concatenate(split(qi[i], PARTS), axis=0)
 
     def project(i):
         if i == 2:
@@ -255,13 +257,10 @@
         sent(Q_BACK, t, qf.at[t, :, 0])
 
 
-def exchange(grads, errors, q0):
+def exchange(*operands):
     vmem = lambda *shape: pltpu.VMEM(shape, F32)
     scratch = [
-        pltpu.VMEM((2, ROWS, D), BF16),
-        pltpu.VMEM((2, ROWS, D), BF16),
-        pltpu.VMEM((D, ROWS), BF16),
-        pltpu.VMEM((D, ROWS), BF16),
+        vmem(3, RANK, D),
         pltpu.VMEM((3, PARTS * RANK, D), BF16),
         vmem(ITERS, 3, 4, 8, ROWS),
         vmem(ITERS, 3, 2, 8, ROWS),
@@ -276,11 +275,11 @@
         vmem(ITERS, 3, NZ, 8, 128),
         vmem(ITERS, 3, 2, 16, 8, 128),
         pltpu.VMEM((3, RANK, 6 * RANK), BF16),
-        pltpu.SemaphoreType.DMA((6,)),
+        pltpu.SemaphoreType.DMA((7,)),
         pltpu.SemaphoreType.DMA((10, ITERS)),
         pltpu.SemaphoreType.DMA((10, ITERS, 3)),
     ]
-    anywhere = pl.BlockSpec(memory_space=pl.ANY)
+    outside = pl.BlockSpec(memory_space=pltpu.HBM)
     inside = pl.BlockSpec(memory_space=pltpu.VMEM)
     return pl.pallas_call(
         kernel,
@@ -289,60 +288,85 @@
             jax.ShapeDtypeStruct((3, RANK, D), F32),
             jax.ShapeDtypeStruct((3, 3 * RANK, ROWS), BF16),
             jax.ShapeDtypeStruct((3, 3 * RANK, D), BF16),
+            jax.ShapeDtypeStruct((2, ROWS, D), BF16),
+            jax.ShapeDtypeStruct((2, ROWS, D), BF16),
+            jax.ShapeDtypeStruct((D, ROWS), BF16),
+            jax.ShapeDtypeStruct((D, ROWS), BF16),
         ),
-        in_specs=[anywhere] * 6 + [inside],
-        out_specs=(inside, inside, inside),
+        in_specs=[outside] * 7,
+        out_specs=(inside,) * 7,
         scratch_shapes=scratch,
         compiler_params=pltpu.CompilerParams(
-            collective_id=0, has_side_effects=True, vmem_limit_bytes=32 << 20
+            collective_id=0, has_side_effects=True, vmem_limit_bytes=24 << 20
         ),
         cost_estimate=pl.CostEstimate(flops=10**9, bytes_accessed=6 * 10**6, transcendentals=0),
-    )(*grads, *errors, q0)
-
-
-STEPS = 4
-WIDE = D // STEPS
-
-
-def finish_kernel(ps, qs, q, g0, g1, g2, e0, e1, e2, u0, u1, u2, n0, n1, n2, q_out):
-    def one(g, e, u, n, left, right):
-        v = dot(left, right, 0, 0)
-        u[...] = v.astype(BF16)
-        n[...] = ((g[...].astype(F32) + e[...].astype(F32)) - v).astype(BF16)
-
-    one(g0, e0, u0, n0, ps[0], qs[0])
-    one(g1, e1, u1, n1, ps[1], qs[1])
-    one(g2, e2, u2, n2, qs[2], ps[2])
-    q_out[...] = q[...]
-
-
-def finish(ps, qs, q, grads, errors):
-    tall = pl.BlockSpec((ROWS, WIDE), lambda s: (0, s))
-    flat = pl.BlockSpec((WIDE, ROWS), lambda s: (s, 0))
-    q_spec = pl.BlockSpec((3, RANK, WIDE), lambda s: (0, 0, s))
+    )(*operands)
+
+
+PIECES = 4
+TALL = ROWS // PIECES
+FLAT = D // PIECES
+
+
+def finish_kernel(ps, qs, q, gm, em, gd, ed, u0, u1, u2, n0, n1, n2, q_out, um, nm, ud, nd, sem):
+    copies = []
+
+    def out(src, dst):
+        cp = pltpu.make_async_copy(src, dst, sem.at[len(copies)])
+        cp.start()
+        copies.append(cp)
+
+    out(q, q_out)
+    for i, (u, n) in enumerate(((u0, n0), (u1, n1))):
+        for k in range(PIECES):
+            rows = pl.ds(k * TALL, TALL)
+            v = dot(ps[i, :, k * TALL : (k + 1) * TALL], qs[i], 0, 0)
+            um[i, rows] = v.astype(BF16)
+            nm[i, rows] = ((gm[i, rows].astype(F32) + em[i, rows].astype(F32)) - v).astype(BF16)
+            out(um.at[i, rows], u.at[rows])
+            out(nm.at[i, rows], n.at[rows])
+    for k in range(PIECES):
+        rows = pl.ds(k * FLAT, FLAT)
+        v = dot(qs[2, :, k * FLAT : (k + 1) * FLAT], ps[2], 0, 0)
+        ud[rows] = v.astype(BF16)
+        nd[rows] = ((gd[rows].astype(F32) + ed[rows].astype(F32)) - v).astype(BF16)
+        out(ud.at[rows], u2.at[rows])
+        out(nd.at[rows], n2.at[rows])
+    for cp in copies:
+        cp.wait()
+
+
+def finish(ps, qs, q, gm, em, gd, ed):
+    inside = pl.BlockSpec(memory_space=pltpu.VMEM)
+    outside = pl.BlockSpec(memory_space=pltpu.HBM)
     shapes = [(ROWS, D), (ROWS, D), (D, ROWS)]
     outs = [jax.ShapeDtypeStruct(shape, BF16) for shape in shapes]
     return pl.pallas_call(
         finish_kernel,
         name="finish",
-        grid=(STEPS,),
-        in_specs=[
-            pl.BlockSpec((3, 3 * RANK, ROWS), lambda s: (0, 0, 0)),
-            pl.BlockSpec((3, 3 * RANK, WIDE), lambda s: (0, 0, s)),
-            q_spec,
-            tall, tall, flat, tall, tall, flat,
+        in_specs=[inside] * 7,
+        out_specs=[outside] * 7,
+        out_shape=outs + outs + [jax.ShapeDtypeStruct((3, RANK, D), F32)],
+        scratch_shapes=[
+            pltpu.VMEM((2, ROWS, D), BF16),
+            pltpu.VMEM((2, ROWS, D), BF16),
+            pltpu.VMEM((D, ROWS), BF16),
+            pltpu.VMEM((D, ROWS), BF16),
+            pltpu.SemaphoreType.DMA((6 * PIECES + 1,)),
         ],
-        out_specs=[tall, tall, flat, tall, tall, flat, q_spec],
-        out_shape=outs + outs + [jax.ShapeDtypeStruct((3, RANK, D), F32)],
-        compiler_params=pltpu.CompilerParams(vmem_limit_bytes=32 << 20),
-    )(ps, qs, q, *grads, *errors)
+        compiler_params=pltpu.CompilerParams(vmem_limit_bytes=24 << 20),
+    )(ps, qs, q, gm, em, gd, ed)
 
 
 def shards(gate_grad, up_grad, down_grad, gate_error, up_error, down_error, q_init):
     grads = (gate_grad[0], up_grad[0], down_grad[0])
     errors = (gate_error[0], up_error[0], down_error[0])
-    q, ps, qs = exchange(grads, errors, jnp.swapaxes(q_init, 1, 2))
-    u0, u1, u2, n0, n1, n2, q_next = finish(ps, qs, q, grads, errors)
+    pinned = [
+        pltpu.with_memory_space_constraint(v, pltpu.HBM)
+        for v in grads + errors + (jnp.swapaxes(q_init, 1, 2),)
+    ]
+    q, ps, qs, *held = exchange(*pinned)
+    u0, u1, u2, n0, n1, n2, q_next = finish(ps, qs, q, *held)
     return u0, u1, u2, n0[None], n1[None], n2[None], jnp.swapaxes(q_next, 1, 2)
 
 

time: 79.5 us -> 70.9 us (0.89)
  local copies, waits for them, and re-layouts: 7.78 us -> 0 us
    unnamed x14 -> x0, local copies, waits for them, and re-layouts: 7.78 us -> none
    pallas_call x1, Pallas kernels: 3.57 us -> 2.66 us  [finish(): pl.pallas_call(finish_kernel, name='finish', in_specs=[inside] * 7, out_s...]
where the time goes in v2:
time: 70.9 us; the launch traced here: 70.8 us
  Pallas kernels  70.1 us (99%)
    pallas_call x1, Pallas kernels, exchange(): pl.pallas_call(kernel, name='power', out_shape=(jax.ShapeDtypeStruct((3,...  67.5 us
    pallas_call x1, Pallas kernels, finish(): pl.pallas_call(finish_kernel, name='finish', in_specs=[inside] * 7, out_s...  2.66 us

profile of v2, /device:TPU:1, one launch (start us, length us, event | category | flops | bytes accessed | tf_op | source)
XLA Modules:
  0.0 70.8 jit_solution(10097630628508197405)
XLA Ops:
  0.6 67.5 %power.1 = (f32[3,32,1024]{2,1,0:T(8,128)S(1)}, bf16[3,96,384]{2,1,0:T(8,128)(2,1)S(1)}, bf16[3,96,1024]{2,1,0:T(8,128)(2,1)S(1)}, bf16[2,384,1024]{2,1,0:T(8,12...) custom-call(bf16[384,1024]{1,0:T(8,128)(2,1)} %bitcast.11, ...), custom_call_target="tpu_custom_call" | custom-call | flops 1000000000 | bytes 6000000 | tf_op jit(solution)/shard_map/power/pallas_call | solution.py:284
  68.1 2.7 %finish.1 = (bf16[384,1024]{1,0:T(8,128)(2,1)}, bf16[384,1024]{1,0:T(8,128)(2,1)}, bf16[1024,384]{1,0:T(8,128)(2,1)}, bf16[384,1024]{1,0:T(8,128)(2,1)}, bf16[38...) custom-call(bf16[3,96,384]{2,1,0:T(8,128)(2,1)S(1)} %get-tuple-element.21.ps, ...), custom_call_target="tpu_custom_call" | custom-call | tf_op jit(solution)/shard_map/finish/pallas_call | solution.py:344

commit v3 on v2

--- a/solution.py
+++ b/solution.py
@@ -73,7 +73,7 @@
     g0, g1, g2, e0, e1, e2, q0,
     q_out, ps_out, qs_out, gm, em, gd, ed,
     qi, qs, pt, pc, x1, x2, pf, gz, qp, qc, qsum, qr, zq, qf, linv,
-    load, ssem, rsem,
+    load, ssem, rsem, know,
 ):
     r = lax.axis_index("replica")
     z = lax.axis_index("tensor")
@@ -97,7 +97,9 @@
     ys = [at((y + d) % NY, x) for d in (2, 1, 3)]
 
     barrier = pltpu.get_barrier_semaphore()
-    greet = [at(yy, xx) for yy, xx in plane] + column + [sib]
+    near = [(r, (z + dz) % NZ) for dz in (1, 7)]
+    next_near = [(r, (z + dz) % NZ) for dz in (2, 6)]
+    greet = xs + ys + near + [sib]
     for dev in greet:
         pl.semaphore_signal(barrier, inc=1, device_id=dev, device_id_type=MESH)
 
@@ -141,15 +143,23 @@
             v = dot(ps, gm[i], 1, 0) + dot(ps, em[i], 1, 0)
         return fold(v, PARTS) * (1.0 / 32.0)
 
+    def tell(k, devs):
+        for dev in devs:
+            pl.semaphore_signal(know.at[k], inc=1, device_id=dev, device_id_type=MESH)
+
+    def project_and_send(t, i):
+        pt[t, i] = project(i).reshape(4, 8, ROWS)
+        if t == 0 and i == 0:
+            pl.semaphore_wait(barrier, len(greet))
+        send(P_CORE, t, i, pt.at[t, i, pl.ds(2 * other, 2)], pc.at[t, i], sib)
+
+    for i in range(3):
+        loads[2 * i].wait()
+        loads[2 * i + 1].wait()
+        project_and_send(0, i)
+    tell(0, near)
+
     def iteration(t, first):
-        for i in range(3):
-            if first:
-                loads[2 * i].wait()
-                loads[2 * i + 1].wait()
-            pt[t, i] = project(i).reshape(4, 8, ROWS)
-            if first and i == 0:
-                pl.semaphore_wait(barrier, len(greet))
-            send(P_CORE, t, i, pt.at[t, i, pl.ds(2 * other, 2)], pc.at[t, i], sib)
         for i in range(3):
             arrived(P_CORE, t, i, pc.at[t, i])
             s = pt[t, i, pl.ds(2 * c, 2)] + pc[t, i]
@@ -169,6 +179,9 @@
                 send(P_TWO, t, i, x2.at[t, i, 0, y], x2.at[t, i, 0, y], dev)
             for dev in xs:
                 send(P_TWO, t, i, x2.at[t, i, 1, x], x2.at[t, i, 1, x], dev)
+        if first:
+            pl.semaphore_wait(know.at[0], 2)
+            tell(1, next_near)
         for i in range(3):
             arrived(P_TWO, t, i, x2.at[t, i, :, pl.ds(0, 3)])
             a = (x2[t, i, 0, 0] + x2[t, i, 0, 1]) + (x2[t, i, 0, 2] + x2[t, i, 0, 3])
@@ -176,6 +189,8 @@
             pf[t, i, 2 * c] = a
             pf[t, i, 2 * c + 1] = b
             send(P_BACK, t, i, pf.at[t, i, pl.ds(2 * c, 2)], pf.at[t, i, pl.ds(2 * c, 2)], sib)
+        if first:
+            pl.semaphore_wait(know.at[1], 2)
         grams = []
         for i in range(3):
             arrived(P_BACK, t, i, pf.at[t, i, pl.ds(0, 2)])
@@ -214,6 +229,11 @@
             qf[t, i, c, p] = jnp.sum(zq[t, i], axis=0)
             for yy, xx in plane:
                 send(Q_GATHER, t, i, qf.at[t, i, c, p], qf.at[t, i, c, p], at(yy, xx))
+        if not first:
+            for i in range(3):
+                p_hat = dot(linv[i], small_right(pf[t, i].reshape(RANK, ROWS)), 1, 0)
+                ph, pw = split(p_hat, 2)
+                ps_out[i] = jnp.concatenate([ph, ph, pw], axis=0)
         for i in range(3):
             arrived(Q_GATHER, t, i, qf.at[t, i, 0, pl.ds(0, 15)])
             send(Q_BACK, t, i, qf.at[t, i, c], qf.at[t, i, c], sib)
@@ -230,13 +250,11 @@
             q_now = dot(linv[i], small_right(raw), 1, 0)
             if first:
                 qs[i] = jnp.concatenate(split(q_now, PARTS), axis=0)
+                project_and_send(t + 1, i)
             else:
                 q_out[i] = q_now
                 qh, ql = split(q_now, 2)
                 qs_out[i] = jnp.concatenate([qh, ql, qh], axis=0)
-                p_hat = dot(linv[i], small_right(pf[t, i].reshape(RANK, ROWS)), 1, 0)
-                ph, pw = split(p_hat, 2)
-                ps_out[i] = jnp.concatenate([ph, ph, pw], axis=0)
 
     for t in range(ITERS):
         iteration(t, t == 0)
@@ -278,6 +296,7 @@
         pltpu.SemaphoreType.DMA((7,)),
         pltpu.SemaphoreType.DMA((10, ITERS)),
         pltpu.SemaphoreType.DMA((10, ITERS, 3)),
+        pltpu.SemaphoreType.REGULAR((2,)),
     ]
     outside = pl.BlockSpec(memory_space=pltpu.HBM)
     inside = pl.BlockSpec(memory_space=pltpu.VMEM)

time: 70.9 us -> 68.8 us (0.970)
  Pallas kernels: 70.1 us -> 68.1 us
    pallas_call x1, Pallas kernels: 67.5 us -> 65.4 us  [exchange(): pl.pallas_call(kernel, name='power', out_shape=(jax.ShapeDtypeStruct((3,...]
where the time goes in v3:
time: 68.8 us; the launch traced here: 68.7 us
  Pallas kernels  68.1 us (99%)
    pallas_call x1, Pallas kernels, exchange(): pl.pallas_call(kernel, name='power', out_shape=(jax.ShapeDtypeStruct((3,...  65.4 us
    pallas_call x1, Pallas kernels, finish(): pl.pallas_call(finish_kernel, name='finish', in_specs=[inside] * 7, out_s...  2.65 us

profile of v3, /device:TPU:1, one launch (start us, length us, event | category | flops | bytes accessed | tf_op | source)
XLA Modules:
  0.0 68.7 jit_solution(1932341781812668291)
XLA Ops:
  0.6 65.4 %power.1 = (f32[3,32,1024]{2,1,0:T(8,128)S(1)}, bf16[3,96,384]{2,1,0:T(8,128)(2,1)S(1)}, bf16[3,96,1024]{2,1,0:T(8,128)(2,1)S(1)}, bf16[2,384,1024]{2,1,0:T(8,12...) custom-call(bf16[384,1024]{1,0:T(8,128)(2,1)} %bitcast.11, ...), custom_call_target="tpu_custom_call" | custom-call | flops 1000000000 | bytes 6000000 | tf_op jit(solution)/shard_map/power/pallas_call | solution.py:303
  66.1 2.6 %finish.1 = (bf16[384,1024]{1,0:T(8,128)(2,1)}, bf16[384,1024]{1,0:T(8,128)(2,1)}, bf16[1024,384]{1,0:T(8,128)(2,1)}, bf16[384,1024]{1,0:T(8,128)(2,1)}, bf16[38...) custom-call(bf16[3,96,384]{2,1,0:T(8,128)(2,1)S(1)} %get-tuple-element.21.ps, ...), custom_call_target="tpu_custom_call" | custom-call | tf_op jit(solution)/shard_map/finish/pallas_call | solution.py:363

commit v4 on v2

v4 whole, which is shorter than its diff:
```python
import jax
import jax.numpy as jnp
from jax import lax
from jax.experimental import pallas as pl
from jax.experimental.pallas import tpu as pltpu
from jax.sharding import PartitionSpec as P

ITERS = 2
D = 1024
RANK = 32
ROWS = 384
NY, NX, NZ = 4, 4, 8
MESH = pl.DeviceIdType.MESH
F32 = jnp.float32
BF16 = jnp.bfloat16
PARTS = 2

(
    P_CORE, P_ONE, P_TWO, P_BACK, GRAM_1, Q_CORE, Q_SCATTER, Q_Z_1, Q_TILE,
    M_CORE, M_A, M_B, M_C,
    P_SUM, P_SHARE, GRAM_2, Q_SUM, Q_Z_2, Q_GATHER, Q_BACK,
) = range(20)
QUART = 96
HALF = 48


def split(x, parts):
    out = []
    for k in range(parts):
        piece = x.astype(BF16)
        out.append(piece)
        if k + 1 < parts:
            x = x - piece.astype(F32)
    return out


def dot(a, b, ca, cb):
    return lax.dot_general(a, b, (((ca,), (cb,)), ((), ())), preferred_element_type=F32)


def small_left(a, cat_axis):
    h, m, l = split(a, 3)
    return jnp.concatenate([h, h, m, h, l, m], axis=cat_axis)


def small_right(b):
    h, m, l = split(b, 3)
    return jnp.concatenate([h, m, h, l, h, m], axis=0)


def fold(x, parts):
    total = x[(parts - 1) * RANK :]
    for k in range(parts - 2, -1, -1):
        total = total + x[k * RANK : (k + 1) * RANK]
    return total


def inverse_factors(grams):
    row = lax.broadcasted_iota(jnp.int32, (RANK, 2 * RANK), 0)
    lane = lax.broadcasted_iota(jnp.int32, (RANK, 2 * RANK), 1)
    eye = (lane == row + RANK).astype(F32)
    augs = []
    for g in grams:
        augs.append(jnp.concatenate([g, jnp.zeros_like(g)], axis=1) + eye)
    for j in range(RANK):
        for n in range(len(augs)):
            a = augs[n]
            pivot = a[j : j + 1, j : j + 1]
            r = lax.rsqrt(pivot)
            r = r * (1.5 - 0.5 * pivot * r * r)
            top = a[j : j + 1, :] * r
            col = a[:, j : j + 1] * r
            a = jnp.where(row > j, a - col * top, jnp.where(row == j, top, a))
            augs[n] = a
    return [a[:, RANK:] for a in augs]


def kernel(
    g0, g1, g2, e0, e1, e2, q0,
    q_out, ps_out, qs_out, gm, em, gd, ed,
    qi, qs, pt, pc, x1, x2, pf, gz, qp, qc, qsum, qr, zq, qt, qtr, linv,
    wb, wr, ra, rb, rc, mean, px, pa, pw, qx, qxr, qf,
    load, ssem, rsem, know,
):
    r = lax.axis_index("replica")
    z = lax.axis_index("tensor")
    y, x, c = r // 8, (r // 2) % 4, r % 2
    p = y * 4 + x
    other = 1 - c
    sib = (y * 8 + x * 2 + other, z)

    def at(yy, xx):
        return (yy * 8 + xx * 2 + c, z)

    plane = [
        ((y + dy) % NY, (x + dx) % NX)
        for dy, dx in [
            (2, 2), (2, 1), (1, 2), (2, 3), (3, 2), (1, 1), (1, 3), (3, 1), (3, 3),
            (2, 0), (0, 2), (1, 0), (0, 1), (3, 0), (0, 3),
        ]
    ]
    column = [(r, (z + dz) % NZ) for dz in (4, 3, 5, 2, 6, 1, 7)]
    xs = [at(y, (x + d) % NX) for d in (2, 1, 3)]
    ys = [at((y + d) % NY, x) for d in (2, 1, 3)]
    yhi, ylo = y // 2, y % 2
    yy1 = yhi * 2 + (1 - ylo)
    rows_group = [at(yy1, (x + d) % NX) for d in (2, 1, 3, 0)] + xs
    yopp = (y + 2) % NY
    lanes_group = [
        (1 - yhi, other, (yopp * 8 + x * 2 + other, z)),
        (1 - yhi, c, at(yopp, x)),
        (yhi, other, sib),
    ]
    rank_group = 2 * c + yhi

    barrier = pltpu.get_barrier_semaphore()
    near = [(r, (z + dz) % NZ) for dz in (1, 7)]
    next_near = [(r, (z + dz) % NZ) for dz in (2, 6)]
    greet = xs + ys + near + [sib]
    for dev in greet:
        pl.semaphore_signal(barrier, inc=1, device_id=dev, device_id_type=MESH)

    loads = []
    for i, (src, dst) in enumerate(
        [(g0, gm.at[0]), (e0, em.at[0]), (g1, gm.at[1]), (e1, em.at[1]), (g2, gd), (e2, ed), (q0, qi)]
    ):
        cp = pltpu.make_async_copy(src, dst, load.at[i])
        loads.append(cp)
    for k in (6, 0, 1, 2, 3, 4, 5):
        loads[k].start()

    def send(stage, i, src, dst, dev):
        pltpu.make_async_remote_copy(
            src_ref=src,
            dst_ref=dst,
            send_sem=ssem.at[stage],
            recv_sem=rsem.at[stage, i],
            device_id=dev,
            device_id_type=MESH,
        ).start()

    def arrived(stage, i, like):
        pltpu.make_async_copy(like, like, rsem.at[stage, i]).wait()

    def sent(stage, like):
        pltpu.make_async_copy(like, like, ssem.at[stage]).wait()

    def tell(k, devs):
        for dev in devs:
            pl.semaphore_signal(know.at[k], inc=1, device_id=dev, device_id_type=MESH)

    place = ((x, y), (y, x))
    step = ((xs[1], xs[2]), (ys[1], ys[2]))
    own = wb.at[c]

    def mean_core(i):
        def put(rows_from, lanes_from, v):
            quarter, h = rows_from // QUART, (rows_from // HALF) % 2
            for k in range(v.shape[1] // 128):
                tile = lanes_from // 128 + k
                ty, tx = (quarter // 2) * 2 + tile // 4, tile % 4
                a, b = (tx, ty) if h == 0 else (ty, tx)
                wb[quarter % 2, i, h, a, b] = v[:, k * 128 : (k + 1) * 128]

        if i == 2:
            for tile in range(8):
                f = slice(tile * 128, (tile + 1) * 128)
                v = (gd[f].astype(F32) + ed[f].astype(F32)) * (1.0 / 32.0)
                v = v.T
                for k in range(8):
                    put(k * HALF, tile * 128, v[k * HALF : (k + 1) * HALF])
        else:
            for k in range(8):
                f = slice(k * HALF, (k + 1) * HALF)
                put(k * HALF, 0, (gm[i, f].astype(F32) + em[i, f].astype(F32)) * (1.0 / 32.0))
        send(M_CORE, i, wb.at[other, i], wr.at[i], sib)

    def mean_a(i):
        arrived(M_CORE, i, wr.at[i])
        wb[c, i] = wb[c, i] + wr[i]
        for h in range(2):
            a, _ = place[h]
            plus, minus = step[h]
            send(M_A, i, own.at[i, h, (a + 2) % 4, pl.ds(0, 2)], ra.at[i, h, 0], plus)
            send(M_A, i, own.at[i, h, (a + 2) % 4, pl.ds(2, 2)], ra.at[i, h, 1], minus)

    def mean_b(i):
        arrived(M_A, i, ra.at[i])
        for h in range(2):
            a, _ = place[h]
            up, down = (a + 1) % 4, (a + 3) % 4
            plus, minus = step[h]
            wb[c, i, h, up, pl.ds(0, 2)] = wb[c, i, h, up, pl.ds(0, 2)] + ra[i, h, 0]
            wb[c, i, h, down, pl.ds(2, 2)] = wb[c, i, h, down, pl.ds(2, 2)] + ra[i, h, 1]
            send(M_B, i, own.at[i, h, up], rb.at[i, h, 0], plus)
            send(M_B, i, own.at[i, h, down], rb.at[i, h, 1], minus)

    def mean_c(i):
        arrived(M_B, i, rb.at[i])
        for h in range(2):
            a, b = place[h]
            wb[c, i, h, a] = wb[c, i, h, a] + rb[i, h, 0] + rb[i, h, 1]
            for k in range(3):
                d = (2, 1, 3)[k]
                dev = (ys, xs)[h][k]
                send(M_C, i, own.at[i, h, a, (b + d) % 4], rc.at[i, h, k], dev)

    def mean_d(i):
        arrived(M_C, i, rc.at[i])
        for h in range(2):
            a, b = place[h]
            v = wb[c, i, h, a, b] + rc[i, h, 0] + (rc[i, h, 1] + rc[i, h, 2])
            hi, lo = split(v, 2)
            mean[i, 0, h * HALF : (h + 1) * HALF] = hi
            mean[i, 1, h * HALF : (h + 1) * HALF] = lo

    loads[6].wait()
    for i in range(3):
        qs[i] = jnp.concatenate(split(qi[i], PARTS), axis=0)

    def project(i):
        if i == 2:
            v = dot(qs[i], gd[...], 1, 0) + dot(qs[i], ed[...], 1, 0)
        else:
            v = dot(qs[i], gm[i], 1, 1) + dot(qs[i], em[i], 1, 1)
        return fold(v, PARTS) * (1.0 / 32.0)

    def back_project(i, ps):
        if i == 2:
            v = dot(ps, gd[...], 1, 1) + dot(ps, ed[...], 1, 1)
        else:
            v = dot(ps, gm[i], 1, 0) + dot(ps, em[i], 1, 0)
        return fold(v, PARTS) * (1.0 / 32.0)

    def gram_of(ps):
        gg = fold(dot(ps, ps, 1, 1), PARTS)
        gram = gg[:, (PARTS - 1) * RANK :]
        for k in range(PARTS - 2, -1, -1):
            gram = gram + gg[:, k * RANK : (k + 1) * RANK]
        return gram

    def gram_send(stage, t, grams):
        gz[t, z] = jnp.concatenate(grams + [jnp.zeros((RANK, RANK), F32)], axis=1)
        for dev in column:
            send(stage, 0, gz.at[t, z], gz.at[t, z], dev)

    def factors(stage, t):
        arrived(stage, 0, gz.at[t, pl.ds(0, 7)])
        gram = jnp.sum(gz[t], axis=0)
        inv = inverse_factors([gram[:, k * RANK : (k + 1) * RANK] for k in range(3)])
        for i in range(3):
            linv[i] = small_left(inv[i], 1)

    for i in range(3):
        loads[2 * i].wait()
        loads[2 * i + 1].wait()
        pt[i] = project(i).reshape(4, 8, ROWS)
        if i == 0:
            pl.semaphore_wait(barrier, len(greet))
        send(P_CORE, i, pt.at[i, pl.ds(2 * other, 2)], pc.at[i], sib)
    tell(0, near)
    mean_core(0)
    mean_core(1)
    for i in range(3):
        arrived(P_CORE, i, pc.at[i])
        s = pt[i, pl.ds(2 * c, 2)] + pc[i]
        x1[i, 0, x] = s[0]
        x1[i, 1, y] = s[1]
        for dev in xs:
            send(P_ONE, i, x1.at[i, 0, x], x1.at[i, 0, x], dev)
        for dev in ys:
            send(P_ONE, i, x1.at[i, 1, y], x1.at[i, 1, y], dev)
    mean_core(2)
    mean_a(0)
    for i in range(3):
        arrived(P_ONE, i, x1.at[i, :, pl.ds(0, 3)])
        a = (x1[i, 0, 0] + x1[i, 0, 1]) + (x1[i, 0, 2] + x1[i, 0, 3])
        b = (x1[i, 1, 0] + x1[i, 1, 1]) + (x1[i, 1, 2] + x1[i, 1, 3])
        x2[i, 0, y] = a
        x2[i, 1, x] = b
        for dev in ys:
            send(P_TWO, i, x2.at[i, 0, y], x2.at[i, 0, y], dev)
        for dev in xs:
            send(P_TWO, i, x2.at[i, 1, x], x2.at[i, 1, x], dev)
    pl.semaphore_wait(know.at[0], 2)
    tell(1, next_near)
    mean_a(1)
    mean_a(2)
    mean_b(0)
    for i in range(3):
        arrived(P_TWO, i, x2.at[i, :, pl.ds(0, 3)])
        a = (x2[i, 0, 0] + x2[i, 0, 1]) + (x2[i, 0, 2] + x2[i, 0, 3])
        b = (x2[i, 1, 0] + x2[i, 1, 1]) + (x2[i, 1, 2] + x2[i, 1, 3])
        pf[i, 2 * c] = a
        pf[i, 2 * c + 1] = b
        send(P_BACK, i, pf.at[i, pl.ds(2 * c, 2)], pf.at[i, pl.ds(2 * c, 2)], sib)
    pl.semaphore_wait(know.at[1], 2)
    grams = []
    for i in range(3):
        arrived(P_BACK, i, pf.at[i, pl.ds(0, 2)])
        ps = jnp.concatenate(split(pf[i].reshape(RANK, ROWS), PARTS), axis=0)
        qp[i] = back_project(i, ps).reshape(2, 2, 8, D)
        send(Q_CORE, i, qp.at[i, other], qc.at[i], sib)
        grams.append(gram_of(ps))
    gram_send(GRAM_1, 0, grams)
    for i in range(3):
        arrived(Q_CORE, i, qc.at[i])
        s = qp[i, c] + qc[i]
        for k in range(16):
            qsum[i, k] = s[k // 8, :, (k % 8) * 128 : (k % 8 + 1) * 128]
        qr[i, p] = qsum[i, p]
        for yy, xx in plane:
            send(Q_SCATTER, i, qsum.at[i, yy * 4 + xx], qr.at[i, p], at(yy, xx))
    mean_b(1)
    mean_b(2)
    for i in range(3):
        arrived(Q_SCATTER, i, qr.at[i, pl.ds(0, 15)])
        zq[0, i, z] = jnp.sum(qr[i], axis=0)
        for dev in column:
            send(Q_Z_1, i, zq.at[0, i, z], zq.at[0, i, z], dev)
    factors(GRAM_1, 0)
    for i in range(3):
        mean_c(i)
    for i in range(3):
        arrived(Q_Z_1, i, zq.at[0, i, pl.ds(0, 7)])
        qt[i, rank_group] = jnp.sum(zq[0, i], axis=0)
        for _, _, dev in lanes_group:
            send(Q_TILE, i, qt.at[i, rank_group], qt.at[i, rank_group], dev)
    for i in range(3):
        arrived(Q_TILE, i, qt.at[i, pl.ds(0, 3)])
        q_now = dot(linv[i], small_right(qt[i].reshape(RANK, 128)), 1, 0)
        qtr[i] = jnp.concatenate(split(q_now, PARTS), axis=0)
    for i in range(3):
        mean_d(i)
        v = fold(dot(qtr[i], mean[i, 0], 1, 1) + dot(qtr[i], mean[i, 1], 1, 1), PARTS)
        slot = ylo * 4 + x
        px[i, slot] = jnp.concatenate([v, jnp.zeros((RANK, 128 - QUART), F32)], axis=1)
        for dev in rows_group:
            send(P_SUM, i, px.at[i, slot], px.at[i, slot], dev)
    for i in range(3):
        arrived(P_SUM, i, px.at[i, pl.ds(0, 7)])
        v = jnp.sum(px[i], axis=0)
        quarter = yhi * 2 + c
        pa[i, quarter] = v
        for _, _, dev in lanes_group:
            send(P_SHARE, i, pa.at[i, quarter], pa.at[i, quarter], dev)
        ps = jnp.concatenate(split(v[:, :QUART], PARTS), axis=0)
        v = fold(dot(ps, mean[i, 0], 1, 0) + dot(ps, mean[i, 1], 1, 0), PARTS)
        qx[i] = v.reshape(4, 8, 128)
        qxr[i, rank_group] = qx[i, rank_group]
        for yh, cc, dev in lanes_group:
            send(Q_SUM, i, qx.at[i, 2 * cc + yh], qxr.at[i, rank_group], dev)
    grams = []
    for i in range(3):
        arrived(P_SHARE, i, pa.at[i, pl.ds(0, 3)])
        whole = jnp.concatenate([pa[i, k][:, :QUART] for k in range(4)], axis=1)
        pw[i] = whole
        grams.append(gram_of(jnp.concatenate(split(whole, PARTS), axis=0)))
    for i in range(3):
        arrived(Q_SUM, i, qxr.at[i, pl.ds(0, 3)])
        zq[1, i, z] = jnp.sum(qxr[i], axis=0)
        for dev in column:
            send(Q_Z_2, i, zq.at[1, i, z], zq.at[1, i, z], dev)
    gram_send(GRAM_2, 1, grams)
    for i in range(3):
        arrived(Q_Z_2, i, zq.at[1, i, pl.ds(0, 7)])
        qf[i, c, p] = jnp.sum(zq[1, i], axis=0)
        for yy, xx in plane:
            send(Q_GATHER, i, qf.at[i, c, p], qf.at[i, c, p], at(yy, xx))
    factors(GRAM_2, 1)
    for i in range(3):
        p_hat = dot(linv[i], small_right(pw[i]), 1, 0)
        ph, p_low = split(p_hat, 2)
        ps_out[i] = jnp.concatenate([ph, ph, p_low], axis=0)
    for i in range(3):
        arrived(Q_GATHER, i, qf.at[i, 0, pl.ds(0, 15)])
        send(Q_BACK, i, qf.at[i, c], qf.at[i, c], sib)
    for i in range(3):
        arrived(Q_BACK, i, qf.at[i, 0])
        full = qf[i]
        raw = jnp.concatenate(
            [
                jnp.concatenate([full[k // 2, (k % 2) * 8 + l] for l in range(8)], axis=1)
                for k in range(4)
            ],
            axis=0,
        )
        q_now = dot(linv[i], small_right(raw), 1, 0)
        q_out[i] = q_now
        qh, ql = split(q_now, 2)
        qs_out[i] = jnp.concatenate([qh, ql, qh], axis=0)

    sent(P_CORE, pc)
    sent(P_ONE, x1.at[:, :, pl.ds(0, 3)])
    sent(P_TWO, x2.at[:, :, pl.ds(0, 3)])
    sent(P_BACK, pf.at[:, pl.ds(0, 2)])
    sent(GRAM_1, gz.at[0, pl.ds(0, 7)])
    sent(Q_CORE, qc)
    sent(Q_SCATTER, qr.at[:, pl.ds(0, 15)])
    sent(Q_Z_1, zq.at[0, :, pl.ds(0, 7)])
    sent(Q_TILE, qt.at[:, pl.ds(0, 3)])
    sent(M_CORE, wr)
    sent(M_A, ra)
    sent(M_B, rb)
    sent(M_C, rc)
    sent(P_SUM, px.at[:, pl.ds(0, 7)])
    sent(P_SHARE, pa.at[:, pl.ds(0, 3)])
    sent(GRAM_2, gz.at[1, pl.ds(0, 7)])
    sent(Q_SUM, qxr.at[:, pl.ds(0, 3)])
    sent(Q_Z_2, zq.at[1, :, pl.ds(0, 7)])
    sent(Q_GATHER, qf.at[:, 0, pl.ds(0, 15)])
    sent(Q_BACK, qf.at[:, 0])


def exchange(*operands):
    vmem = lambda *shape: pltpu.VMEM(shape, F32)
    scratch = [
        vmem(3, RANK, D),
        pltpu.VMEM((3, PARTS * RANK, D), BF16),
        vmem(3, 4, 8, ROWS),
        vmem(3, 2, 8, ROWS),
        vmem(3, 2, 4, 8, ROWS),
        vmem(3, 2, 4, 8, ROWS),
        vmem(3, 4, 8, ROWS),
        vmem(ITERS, NZ, RANK, 128),
        vmem(3, 2, 2, 8, D),
        vmem(3, 2, 8, D),
        vmem(3, 16, 8, 128),
        vmem(3, 16, 8, 128),
        vmem(ITERS, 3, NZ, 8, 128),
        vmem(3, 4, 8, 128),
        pltpu.VMEM((3, PARTS * RANK, 128), BF16),
        pltpu.VMEM((3, RANK, 6 * RANK), BF16),
        vmem(2, 3, 2, 4, 4, HALF, 128),
        vmem(3, 2, 4, 4, HALF, 128),
        vmem(3, 2, 2, 2, HALF, 128),
        vmem(3, 2, 2, 4, HALF, 128),
        vmem(3, 2, 3, HALF, 128),
        pltpu.VMEM((3, 2, QUART, 128), BF16),
        vmem(3, 8, RANK, 128),
        vmem(3, 4, RANK, 128),
        vmem(3, RANK, ROWS),
        vmem(3, 4, 8, 128),
        vmem(3, 4, 8, 128),
        vmem(3, 2, 16, 8, 128),
        pltpu.SemaphoreType.DMA((7,)),
        pltpu.SemaphoreType.DMA((20,)),
        pltpu.SemaphoreType.DMA((20, 3)),
        pltpu.SemaphoreType.REGULAR((2,)),
    ]
    inside = pl.BlockSpec(memory_space=pltpu.VMEM)
    outside = pl.BlockSpec(memory_space=pltpu.HBM)
    return pl.pallas_call(
        kernel,
        name="power",
        out_shape=(
            jax.ShapeDtypeStruct((3, RANK, D), F32),
            jax.ShapeDtypeStruct((3, 3 * RANK, ROWS), BF16),
            jax.ShapeDtypeStruct((3, 3 * RANK, D), BF16),
            jax.ShapeDtypeStruct((2, ROWS, D), BF16),
            jax.ShapeDtypeStruct((2, ROWS, D), BF16),
            jax.ShapeDtypeStruct((D, ROWS), BF16),
            jax.ShapeDtypeStruct((D, ROWS), BF16),
        ),
        in_specs=[outside] * 7,
        out_specs=(inside,) * 7,
        scratch_shapes=scratch,
        compiler_params=pltpu.CompilerParams(
            collective_id=0, has_side_effects=True, vmem_limit_bytes=32 << 20
        ),
        cost_estimate=pl.CostEstimate(flops=10**9, bytes_accessed=6 * 10**6, transcendentals=0),
    )(*operands)


PIECES = 4
TALL = ROWS // PIECES
FLAT = D // PIECES


def finish_kernel(ps, qs, q, gm, em, gd, ed, u0, u1, u2, n0, n1, n2, q_out, um, nm, ud, nd, sem):
    copies = []

    def out(src, dst):
        cp = pltpu.make_async_copy(src, dst, sem.at[len(copies)])
        cp.start()
        copies.append(cp)

    out(q, q_out)
    for i, (u, n) in enumerate(((u0, n0), (u1, n1))):
        for k in range(PIECES):
            rows = pl.ds(k * TALL, TALL)
            v = dot(ps[i, :, k * TALL : (k + 1) * TALL], qs[i], 0, 0)
            um[i, rows] = v.astype(BF16)
            nm[i, rows] = ((gm[i, rows].astype(F32) + em[i, rows].astype(F32)) - v).astype(BF16)
            out(um.at[i, rows], u.at[rows])
            out(nm.at[i, rows], n.at[rows])
    for k in range(PIECES):
        rows = pl.ds(k * FLAT, FLAT)
        v = dot(qs[2, :, k * FLAT : (k + 1) * FLAT], ps[2], 0, 0)
        ud[rows] = v.astype(BF16)
        nd[rows] = ((gd[rows].astype(F32) + ed[rows].astype(F32)) - v).astype(BF16)
        out(ud.at[rows], u2.at[rows])
        out(nd.at[rows], n2.at[rows])
    for cp in copies:
        cp.wait()


def finish(ps, qs, q, gm, em, gd, ed):
    inside = pl.BlockSpec(memory_space=pltpu.VMEM)
    outside = pl.BlockSpec(memory_space=pltpu.HBM)
    shapes = [(ROWS, D), (ROWS, D), (D, ROWS)]
    outs = [jax.ShapeDtypeStruct(shape, BF16) for shape in shapes]
    return pl.pallas_call(
        finish_kernel,
        name="finish",
        in_specs=[inside] * 7,
        out_specs=[outside] * 7,
        out_shape=outs + outs + [jax.ShapeDtypeStruct((3, RANK, D), F32)],
        scratch_shapes=[
            pltpu.VMEM((2, ROWS, D), BF16),
            pltpu.VMEM((2, ROWS, D), BF16),
            pltpu.VMEM((D, ROWS), BF16),
            pltpu.VMEM((D, ROWS), BF16),
            pltpu.SemaphoreType.DMA((6 * PIECES + 1,)),
        ],
        compiler_params=pltpu.CompilerParams(vmem_limit_bytes=24 << 20),
    )(ps, qs, q, gm, em, gd, ed)


def shards(gate_grad, up_grad, down_grad, gate_error, up_error, down_error, q_init):
    grads = (gate_grad[0], up_grad[0], down_grad[0])
    errors = (gate_error[0], up_error[0], down_error[0])
    pinned = [
        pltpu.with_memory_space_constraint(v, pltpu.HBM)
        for v in grads + errors + (jnp.swapaxes(q_init, 1, 2),)
    ]
    q, ps, qs, *held = exchange(*pinned)
    u0, u1, u2, n0, n1, n2, q_next = finish(ps, qs, q, *held)
    return u0, u1, u2, n0[None], n1[None], n2[None], jnp.swapaxes(q_next, 1, 2)


def solution(mesh):
    in_specs = (
        P("replica", "tensor", None),
        P("replica", "tensor", None),
        P("replica", None, "tensor"),
        P("replica", "tensor", None),
        P("replica", "tensor", None),
        P("replica", None, "tensor"),
        P(),
    )
    out_specs = (
        P("tensor", None),
        P("tensor", None),
        P(None, "tensor"),
        P("replica", "tensor", None),
        P("replica", "tensor", None),
        P("replica", None, "tensor"),
        P(),
    )
    return jax.shard_map(shards, mesh=mesh, in_specs=in_specs, out_specs=out_specs, check_vma=False)
```

time: 70.9 us -> 64.3 us (0.907)
  Pallas kernels: 70.1 us -> 63.6 us
    pallas_call x1, Pallas kernels: 67.5 us -> 60.9 us  [exchange(): pl.pallas_call(kernel, name='power', out_shape=(jax.ShapeDtypeStruct((3,...]
where the time goes in v4:
time: 64.3 us; the launch traced here: 64.2 us
  Pallas kernels  63.6 us (99%)
    pallas_call x1, Pallas kernels, exchange(): pl.pallas_call(kernel, name='power', out_shape=(jax.ShapeDtypeStruct((3,...  60.9 us
    pallas_call x1, Pallas kernels, finish(): pl.pallas_call(finish_kernel, name='finish', in_specs=[inside] * 7, out_s...  2.65 us

profile of v4, /device:TPU:1, one launch (start us, length us, event | category | flops | bytes accessed | tf_op | source)
XLA Modules:
  0.0 64.2 jit_solution(17602436585439512630)
XLA Ops:
  0.6 60.9 %power.1 = (f32[3,32,1024]{2,1,0:T(8,128)S(1)}, bf16[3,96,384]{2,1,0:T(8,128)(2,1)S(1)}, bf16[3,96,1024]{2,1,0:T(8,128)(2,1)S(1)}, bf16[2,384,1024]{2,1,0:T(8,12...) custom-call(bf16[384,1024]{1,0:T(8,128)(2,1)} %bitcast.11, ...), custom_call_target="tpu_custom_call" | custom-call | flops 1000000000 | bytes 6000000 | tf_op jit(solution)/shard_map/power/pallas_call | solution.py:453
  61.6 2.7 %finish.1 = (bf16[384,1024]{1,0:T(8,128)(2,1)}, bf16[384,1024]{1,0:T(8,128)(2,1)}, bf16[1024,384]{1,0:T(8,128)(2,1)}, bf16[384,1024]{1,0:T(8,128)(2,1)}, bf16[38...) custom-call(bf16[3,96,384]{2,1,0:T(8,128)(2,1)S(1)} %get-tuple-element.21.ps, ...), custom_call_target="tpu_custom_call" | custom-call | tf_op jit(solution)/shard_map/finish/pallas_call | solution.py:513

commit v5 on v4

--- a/solution.py
+++ b/solution.py
@@ -46,6 +46,16 @@
 def small_right(b):
     h, m, l = split(b, 3)
     return jnp.concatenate([h, m, h, l, h, m], axis=0)
+
+
+def pack(v):
+    tail = jnp.concatenate([v[24:, k * 32 : (k + 1) * 32] for k in range(3)], axis=0)
+    return jnp.concatenate([v[:24], tail], axis=1)
+
+
+def unpack(v):
+    tail = jnp.concatenate([v[8 * k : 8 * k + 8, QUART:] for k in range(3)], axis=1)
+    return jnp.concatenate([v[:, :QUART], tail], axis=0)
 
 
 def fold(x, parts):
@@ -85,7 +95,7 @@
     r = lax.axis_index("replica")
     z = lax.axis_index("tensor")
     y, x, c = r // 8, (r // 2) % 4, r % 2
-    p = y * 4 + x
+    ps_index = (y * 4 + x, x * 4 + y, y * 4 + x)
     other = 1 - c
     sib = (y * 8 + x * 2 + other, z)
 
@@ -102,16 +112,22 @@
     column = [(r, (z + dz) % NZ) for dz in (4, 3, 5, 2, 6, 1, 7)]
     xs = [at(y, (x + d) % NX) for d in (2, 1, 3)]
     ys = [at((y + d) % NY, x) for d in (2, 1, 3)]
-    yhi, ylo = y // 2, y % 2
-    yy1 = yhi * 2 + (1 - ylo)
-    rows_group = [at(yy1, (x + d) % NX) for d in (2, 1, 3, 0)] + xs
-    yopp = (y + 2) % NY
-    lanes_group = [
-        (1 - yhi, other, (yopp * 8 + x * 2 + other, z)),
-        (1 - yhi, c, at(yopp, x)),
-        (yhi, other, sib),
-    ]
-    rank_group = 2 * c + yhi
+    yflip, xflip = (y // 2) * 2 + (1 - y % 2), (x // 2) * 2 + (1 - x % 2)
+    along_x = [at(yflip, (x + d) % NX) for d in (2, 1, 3, 0)] + xs
+    along_y = [at((y + d) % NY, xflip) for d in (2, 1, 3, 0)] + ys
+    rows_group = (along_x, along_y, along_x)
+    yopp, xopp = (y + 2) % NY, (x + 2) % NX
+
+    def four(high, yy, xx):
+        return [
+            (1 - high, other, (yy * 8 + xx * 2 + other, z)),
+            (1 - high, c, at(yy, xx)),
+            (high, other, sib),
+        ]
+
+    lanes_group = (four(y // 2, yopp, x), four(x // 2, y, xopp), four(y // 2, yopp, x))
+    highs, slots = (y // 2, x // 2, y // 2), ((y % 2) * 4 + x, (x % 2) * 4 + y, (y % 2) * 4 + x)
+    rank_groups = [2 * c + high for high in highs]
 
     barrier = pltpu.get_barrier_semaphore()
     near = [(r, (z + dz) % NZ) for dz in (1, 7)]
@@ -159,7 +175,7 @@
             for k in range(v.shape[1] // 128):
                 tile = lanes_from // 128 + k
                 ty, tx = (quarter // 2) * 2 + tile // 4, tile % 4
-                a, b = (tx, ty) if h == 0 else (ty, tx)
+                a, b = (tx, ty) if (h == 0) == (i != 1) else (ty, tx)
                 wb[quarter % 2, i, h, a, b] = v[:, k * 128 : (k + 1) * 128]
 
         if i == 2:
@@ -260,7 +276,6 @@
         send(P_CORE, i, pt.at[i, pl.ds(2 * other, 2)], pc.at[i], sib)
     tell(0, near)
     mean_core(0)
-    mean_core(1)
     for i in range(3):
         arrived(P_CORE, i, pc.at[i])
         s = pt[i, pl.ds(2 * c, 2)] + pc[i]
@@ -270,6 +285,7 @@
             send(P_ONE, i, x1.at[i, 0, x], x1.at[i, 0, x], dev)
         for dev in ys:
             send(P_ONE, i, x1.at[i, 1, y], x1.at[i, 1, y], dev)
+    mean_core(1)
     mean_core(2)
     mean_a(0)
     for i in range(3):
@@ -308,9 +324,11 @@
         s = qp[i, c] + qc[i]
         for k in range(16):
             qsum[i, k] = s[k // 8, :, (k % 8) * 128 : (k % 8 + 1) * 128]
+        p = ps_index[i]
         qr[i, p] = qsum[i, p]
         for yy, xx in plane:
-            send(Q_SCATTER, i, qsum.at[i, yy * 4 + xx], qr.at[i, p], at(yy, xx))
+            there = xx * 4 + yy if i == 1 else yy * 4 + xx
+            send(Q_SCATTER, i, qsum.at[i, there], qr.at[i, p], at(yy, xx))
     mean_b(1)
     mean_b(2)
     for i in range(3):
@@ -318,52 +336,55 @@
         zq[0, i, z] = jnp.sum(qr[i], axis=0)
         for dev in column:
             send(Q_Z_1, i, zq.at[0, i, z], zq.at[0, i, z], dev)
+    mean_c(0)
     factors(GRAM_1, 0)
-    for i in range(3):
+    for i in range(1, 3):
         mean_c(i)
     for i in range(3):
         arrived(Q_Z_1, i, zq.at[0, i, pl.ds(0, 7)])
-        qt[i, rank_group] = jnp.sum(zq[0, i], axis=0)
-        for _, _, dev in lanes_group:
-            send(Q_TILE, i, qt.at[i, rank_group], qt.at[i, rank_group], dev)
+        qt[i, rank_groups[i]] = jnp.sum(zq[0, i], axis=0)
+        for _, _, dev in lanes_group[i]:
+            send(Q_TILE, i, qt.at[i, rank_groups[i]], qt.at[i, rank_groups[i]], dev)
     for i in range(3):
         arrived(Q_TILE, i, qt.at[i, pl.ds(0, 3)])
         q_now = dot(linv[i], small_right(qt[i].reshape(RANK, 128)), 1, 0)
         qtr[i] = jnp.concatenate(split(q_now, PARTS), axis=0)
-    for i in range(3):
         mean_d(i)
         v = fold(dot(qtr[i], mean[i, 0], 1, 1) + dot(qtr[i], mean[i, 1], 1, 1), PARTS)
-        slot = ylo * 4 + x
-        px[i, slot] = jnp.concatenate([v, jnp.zeros((RANK, 128 - QUART), F32)], axis=1)
-        for dev in rows_group:
+        slot = slots[i]
+        px[i, slot] = pack(v)
+        for dev in rows_group[i]:
             send(P_SUM, i, px.at[i, slot], px.at[i, slot], dev)
     for i in range(3):
         arrived(P_SUM, i, px.at[i, pl.ds(0, 7)])
         v = jnp.sum(px[i], axis=0)
-        quarter = yhi * 2 + c
+        quarter = highs[i] * 2 + c
         pa[i, quarter] = v
-        for _, _, dev in lanes_group:
-            send(P_SHARE, i, pa.at[i, quarter], pa.at[i, quarter], dev)
-        ps = jnp.concatenate(split(v[:, :QUART], PARTS), axis=0)
+        ps = jnp.concatenate(split(unpack(v), PARTS), axis=0)
         v = fold(dot(ps, mean[i, 0], 1, 0) + dot(ps, mean[i, 1], 1, 0), PARTS)
         qx[i] = v.reshape(4, 8, 128)
-        qxr[i, rank_group] = qx[i, rank_group]
-        for yh, cc, dev in lanes_group:
-            send(Q_SUM, i, qx.at[i, 2 * cc + yh], qxr.at[i, rank_group], dev)
-    grams = []
-    for i in range(3):
-        arrived(P_SHARE, i, pa.at[i, pl.ds(0, 3)])
-        whole = jnp.concatenate([pa[i, k][:, :QUART] for k in range(4)], axis=1)
-        pw[i] = whole
-        grams.append(gram_of(jnp.concatenate(split(whole, PARTS), axis=0)))
+        qxr[i, rank_groups[i]] = qx[i, rank_groups[i]]
+        for yh, cc, dev in lanes_group[i]:
+            send(Q_SUM, i, qx.at[i, 2 * cc + yh], qxr.at[i, rank_groups[i]], dev)
+    for i in range(3):
+        quarter = highs[i] * 2 + c
+        for _, _, dev in lanes_group[i]:
+            send(P_SHARE, i, pa.at[i, quarter], pa.at[i, quarter], dev)
     for i in range(3):
         arrived(Q_SUM, i, qxr.at[i, pl.ds(0, 3)])
         zq[1, i, z] = jnp.sum(qxr[i], axis=0)
         for dev in column:
             send(Q_Z_2, i, zq.at[1, i, z], zq.at[1, i, z], dev)
+    grams = []
+    for i in range(3):
+        arrived(P_SHARE, i, pa.at[i, pl.ds(0, 3)])
+        whole = jnp.concatenate([unpack(pa[i, k]) for k in range(4)], axis=1)
+        pw[i] = whole
+        grams.append(gram_of(jnp.concatenate(split(whole, PARTS), axis=0)))
     gram_send(GRAM_2, 1, grams)
     for i in range(3):
         arrived(Q_Z_2, i, zq.at[1, i, pl.ds(0, 7)])
+        p = ps_index[i]
         qf[i, c, p] = jnp.sum(zq[1, i], axis=0)
         for yy, xx in plane:
             send(Q_GATHER, i, qf.at[i, c, p], qf.at[i, c, p], at(yy, xx))
@@ -437,8 +458,8 @@
         vmem(3, 2, 2, 4, HALF, 128),
         vmem(3, 2, 3, HALF, 128),
         pltpu.VMEM((3, 2, QUART, 128), BF16),
-        vmem(3, 8, RANK, 128),
-        vmem(3, 4, RANK, 128),
+        vmem(3, 8, 24, 128),
+        vmem(3, 4, 24, 128),
         vmem(3, RANK, ROWS),
         vmem(3, 4, 8, 128),
         vmem(3, 4, 8, 128),

time: 64.3 us -> 61.3 us (0.953)
  Pallas kernels: 63.6 us -> 60.6 us
    pallas_call x1, Pallas kernels: 60.9 us -> 57.9 us  [exchange(): pl.pallas_call(kernel, name='power', out_shape=(jax.ShapeDtypeStruct((3,...]
where the time goes in v5:
time: 61.3 us; the launch traced here: 61.2 us
  Pallas kernels  60.6 us (99%)
  between operations  0.64 us (1%)
    pallas_call x1, Pallas kernels, exchange(): pl.pallas_call(kernel, name='power', out_shape=(jax.ShapeDtypeStruct((3,...  57.9 us
    pallas_call x1, Pallas kernels, finish(): pl.pallas_call(finish_kernel, name='finish', in_specs=[inside] * 7, out_s...  2.65 us

profile of v5, /device:TPU:1, one launch (start us, length us, event | category | flops | bytes accessed | tf_op | source)
XLA Modules:
  0.0 61.2 jit_solution(14397449937365868416)
XLA Ops:
  0.6 57.9 %power.1 = (f32[3,32,1024]{2,1,0:T(8,128)S(1)}, bf16[3,96,384]{2,1,0:T(8,128)(2,1)S(1)}, bf16[3,96,1024]{2,1,0:T(8,128)(2,1)S(1)}, bf16[2,384,1024]{2,1,0:T(8,12...) custom-call(bf16[384,1024]{1,0:T(8,128)(2,1)} %bitcast.11, ...), custom_call_target="tpu_custom_call" | custom-call | flops 1000000000 | bytes 6000000 | tf_op jit(solution)/shard_map/power/pallas_call | solution.py:474
  58.6 2.7 %finish.1 = (bf16[384,1024]{1,0:T(8,128)(2,1)}, bf16[384,1024]{1,0:T(8,128)(2,1)}, bf16[1024,384]{1,0:T(8,128)(2,1)}, bf16[384,1024]{1,0:T(8,128)(2,1)}, bf16[38...) custom-call(bf16[3,96,384]{2,1,0:T(8,128)(2,1)S(1)} %get-tuple-element.21.ps, ...), custom_call_target="tpu_custom_call" | custom-call | tf_op jit(solution)/shard_map/finish/pallas_call | solution.py:534

commit v6 on v5

--- a/solution.py
+++ b/solution.py
@@ -87,8 +87,8 @@
 
 def kernel(
     g0, g1, g2, e0, e1, e2, q0,
-    q_out, ps_out, qs_out, gm, em, gd, ed,
-    qi, qs, pt, pc, x1, x2, pf, gz, qp, qc, qsum, qr, zq, qt, qtr, linv,
+    q_out, ps_out, qs_out, mm, md,
+    gm, em, gd, ed, qi, qs, pt, pc, x1, x2, pf, gz, qp, qc, qsum, qr, zq, qt, qtr, linv,
     wb, wr, ra, rb, rc, mean, px, pa, pw, qx, qxr, qf,
     load, ssem, rsem, know,
 ):
@@ -181,14 +181,17 @@
         if i == 2:
             for tile in range(8):
                 f = slice(tile * 128, (tile + 1) * 128)
-                v = (gd[f].astype(F32) + ed[f].astype(F32)) * (1.0 / 32.0)
-                v = v.T
+                v = gd[f].astype(F32) + ed[f].astype(F32)
+                md[f] = v
+                v = (v * (1.0 / 32.0)).T
                 for k in range(8):
                     put(k * HALF, tile * 128, v[k * HALF : (k + 1) * HALF])
         else:
             for k in range(8):
                 f = slice(k * HALF, (k + 1) * HALF)
-                put(k * HALF, 0, (gm[i, f].astype(F32) + em[i, f].astype(F32)) * (1.0 / 32.0))
+                v = gm[i, f].astype(F32) + em[i, f].astype(F32)
+                mm[i, f] = v
+                put(k * HALF, 0, v * (1.0 / 32.0))
         send(M_CORE, i, wb.at[other, i], wr.at[i], sib)
 
     def mean_a(i):
@@ -390,12 +393,12 @@
             send(Q_GATHER, i, qf.at[i, c, p], qf.at[i, c, p], at(yy, xx))
     factors(GRAM_2, 1)
     for i in range(3):
+        arrived(Q_GATHER, i, qf.at[i, 0, pl.ds(0, 15)])
+        send(Q_BACK, i, qf.at[i, c], qf.at[i, c], sib)
+    for i in range(3):
         p_hat = dot(linv[i], small_right(pw[i]), 1, 0)
         ph, p_low = split(p_hat, 2)
         ps_out[i] = jnp.concatenate([ph, ph, p_low], axis=0)
-    for i in range(3):
-        arrived(Q_GATHER, i, qf.at[i, 0, pl.ds(0, 15)])
-        send(Q_BACK, i, qf.at[i, c], qf.at[i, c], sib)
     for i in range(3):
         arrived(Q_BACK, i, qf.at[i, 0])
         full = qf[i]
@@ -436,6 +439,10 @@
 def exchange(*operands):
     vmem = lambda *shape: pltpu.VMEM(shape, F32)
     scratch = [
+        pltpu.VMEM((2, ROWS, D), BF16),
+        pltpu.VMEM((2, ROWS, D), BF16),
+        pltpu.VMEM((D, ROWS), BF16),
+        pltpu.VMEM((D, ROWS), BF16),
         vmem(3, RANK, D),
         pltpu.VMEM((3, PARTS * RANK, D), BF16),
         vmem(3, 4, 8, ROWS),
@@ -478,13 +485,11 @@
             jax.ShapeDtypeStruct((3, RANK, D), F32),
             jax.ShapeDtypeStruct((3, 3 * RANK, ROWS), BF16),
             jax.ShapeDtypeStruct((3, 3 * RANK, D), BF16),
-            jax.ShapeDtypeStruct((2, ROWS, D), BF16),
-            jax.ShapeDtypeStruct((2, ROWS, D), BF16),
-            jax.ShapeDtypeStruct((D, ROWS), BF16),
-            jax.ShapeDtypeStruct((D, ROWS), BF16),
+            jax.ShapeDtypeStruct((2, ROWS, D), F32),
+            jax.ShapeDtypeStruct((D, ROWS), F32),
         ),
         in_specs=[outside] * 7,
-        out_specs=(inside,) * 7,
+        out_specs=(inside,) * 5,
         scratch_shapes=scratch,
         compiler_params=pltpu.CompilerParams(
             collective_id=0, has_side_effects=True, vmem_limit_bytes=32 << 20
@@ -498,7 +503,7 @@
 FLAT = D // PIECES
 
 
-def finish_kernel(ps, qs, q, gm, em, gd, ed, u0, u1, u2, n0, n1, n2, q_out, um, nm, ud, nd, sem):
+def finish_kernel(ps, qs, q, mm, md, u0, u1, u2, n0, n1, n2, q_out, um, nm, ud, nd, sem):
     copies = []
 
     def out(src, dst):
@@ -512,21 +517,21 @@
             rows = pl.ds(k * TALL, TALL)
             v = dot(ps[i, :, k * TALL : (k + 1) * TALL], qs[i], 0, 0)
             um[i, rows] = v.astype(BF16)
-            nm[i, rows] = ((gm[i, rows].astype(F32) + em[i, rows].astype(F32)) - v).astype(BF16)
+            nm[i, rows] = (mm[i, rows] - v).astype(BF16)
             out(um.at[i, rows], u.at[rows])
             out(nm.at[i, rows], n.at[rows])
     for k in range(PIECES):
         rows = pl.ds(k * FLAT, FLAT)
         v = dot(qs[2, :, k * FLAT : (k + 1) * FLAT], ps[2], 0, 0)
         ud[rows] = v.astype(BF16)
-        nd[rows] = ((gd[rows].astype(F32) + ed[rows].astype(F32)) - v).astype(BF16)
+        nd[rows] = (md[rows] - v).astype(BF16)
         out(ud.at[rows], u2.at[rows])
         out(nd.at[rows], n2.at[rows])
     for cp in copies:
         cp.wait()
 
 
-def finish(ps, qs, q, gm, em, gd, ed):
+def finish(ps, qs, q, mm, md):
     inside = pl.BlockSpec(memory_space=pltpu.VMEM)
     outside = pl.BlockSpec(memory_space=pltpu.HBM)
     shapes = [(ROWS, D), (ROWS, D), (D, ROWS)]
@@ -534,7 +539,7 @@
     return pl.pallas_call(
         finish_kernel,
         name="finish",
-        in_specs=[inside] * 7,
+        in_specs=[inside] * 5,
         out_specs=[outside] * 7,
         out_shape=outs + outs + [jax.ShapeDtypeStruct((3, RANK, D), F32)],
         scratch_shapes=[
@@ -545,7 +550,7 @@
             pltpu.SemaphoreType.DMA((6 * PIECES + 1,)),
         ],
         compiler_params=pltpu.CompilerParams(vmem_limit_bytes=24 << 20),
-    )(ps, qs, q, gm, em, gd, ed)
+    )(ps, qs, q, mm, md)
 
 
 def shards(gate_grad, up_grad, down_grad, gate_error, up_error, down_error, q_init):

time: 61.3 us -> 61.2 us (level)
  no operation moved by 1% of the time
where the time goes in v6:
time: 61.2 us; the launch traced here: 61.1 us
  Pallas kernels  60.4 us (99%)
  between operations  0.64 us (1%)
    pallas_call x1, Pallas kernels, exchange(): pl.pallas_call(kernel, name='power', out_shape=(jax.ShapeDtypeStruct((3,...  57.8 us
    pallas_call x1, Pallas kernels, finish(): pl.pallas_call(finish_kernel, name='finish', in_specs=[inside] * 5, out_s...  2.63 us

profile of v6, /device:TPU:1, one launch (start us, length us, event | category | flops | bytes accessed | tf_op | source)
XLA Modules:
  0.0 61.1 jit_solution(16437199799746252993)
XLA Ops:
  0.6 57.8 %power.1 = (f32[3,32,1024]{2,1,0:T(8,128)S(1)}, bf16[3,96,384]{2,1,0:T(8,128)(2,1)S(1)}, bf16[3,96,1024]{2,1,0:T(8,128)(2,1)S(1)}, f32[2,384,1024]{2,1,0:T(8,128)S(1)}, f32[1024,384]{1,0:T(8,128)S(1)}) custom-call(bf16[384,1024]{1,0:T(8,128)(2,1)} %bitcast.11, bf16[384,1024]{1,0:T(8,128)(2,1)} %bitcast.12, bf16[1024,384]{1,0:T(8,128)(2,1)} %bitcast.13, ...), custom_call_target="tpu_custom_call" | custom-call | flops 1000000000 | bytes 6000000 | tf_op jit(solution)/shard_map/power/pallas_call | solution.py:481
  58.4 2.6 %finish.1 = (bf16[384,1024]{1,0:T(8,128)(2,1)}, bf16[384,1024]{1,0:T(8,128)(2,1)}, bf16[1024,384]{1,0:T(8,128)(2,1)}, bf16[384,1024]{1,0:T(8,128)(2,1)}, bf16[38...) custom-call(bf16[3,96,384]{2,1,0:T(8,128)(2,1)S(1)} %get-tuple-element.19.ps, ...), custom_call_target="tpu_custom_call" | custom-call | tf_op jit(solution)/shard_map/finish/pallas_call | solution.py:539
